TPU v7x, 32 devices: a whole 2x2x4 slice. The times are simulated.
32 devices in a mesh: wide: 16 (over z, y, x), narrow: 2 (over core).
Axes of the slice: x: 2, y: 2, z: 4, core: 2. Of those that a mesh axis runs over, the one named last changes fastest.
Arguments:
- hidden: bfloat16 [512, 8192], P('wide', 'narrow'), may hold values from -6 to 6
- norm_gain: float32 [8192], P('narrow'), may hold values from 0.1 to 1.9
- head_weight: bfloat16 [8192, 32000], P('narrow', 'wide'), may hold values from -0.24 to 0.24
- diff_rows: bfloat16 [16, 2, 8, 32000], P('wide', 'narrow'), may hold values from -6 to 480
- slot_request: int32 [16, 2, 8], replicated, may hold values from 0 to 511, as said below
- slot_code: int32 [16, 2, 8], replicated, may hold values from 1 to 8
- slot_count: int32 [16, 2], replicated, may hold values from 1 to 8, as said below
Outputs:
- log_probs: float32 [512, 32000], P('narrow', 'wide')
Inputs may be any that keep to these rules, and one draw needn't show every extreme that they name: `slot_request`: within one pair, every request is named at most once. `slot_count`: slots at or beyond the count hold no row to use; in every draw some device uses all 8 slots.
All inputs are finite; a program needn't handle non-finite values.
Results may differ from a plain program's by a relative error of at most 0.0003.
Values may be sent and summed in bfloat16 or wider, within the bound.
No kernel may reach another device: no remote copies, remote signals or barrier semaphores. Data moves between devices by JAX's collectives and lax.ppermute only.
A program may use at most 64 MiB of HBM per device.

v0:
```python
import jax
import jax.numpy as jnp
from jax import lax
from jax.sharding import PartitionSpec as P

D = 8192


epsilon = 1e-05


def combined_all(part, axis, combine):
    gathered = jax.tree.map(lambda a: lax.all_gather(a, axis), part)

    def take(source):
        return jax.tree.map(lambda a: lax.dynamic_index_in_dim(a, source, 0, False), gathered)

    return lax.fori_loop(
        1, lax.axis_size(axis), lambda source, state: combine(state, take(source)), take(0)
    )


def merge_pair(earlier, later):
    row_peak = jnp.maximum(earlier[0], later[0])
    summed = earlier[1] * jnp.exp(earlier[0] - row_peak) + later[1] * jnp.exp(later[0] - row_peak)
    return (row_peak, summed)


def body(hidden, norm_gain, head_weight, diff_rows, slot_request, slot_code, slot_count):
    values = hidden.astype(jnp.float32)
    squares = lax.psum(jnp.sum(values * values, axis=1), "narrow")
    scales = lax.rsqrt(squares / D + epsilon)
    normed = (values * scales[:, None] * norm_gain[None, :]).astype(jnp.bfloat16)
    partial_value = jnp.dot(
        lax.all_gather(normed, "wide", axis=0, tiled=True),
        head_weight,
        preferred_element_type=jnp.float32,
    )
    row_block = diff_rows[0, 0]
    arrived = lax.all_to_all(row_block, "wide", split_axis=1, concat_axis=0, tiled=True)
    slot_total = row_block.shape[0]
    active = jnp.arange(slot_total, dtype=jnp.int32)[None, None, :] < slot_count[:, :, None]
    weights = jnp.where(active, slot_code, 0).astype(jnp.float32) * 0.25
    base_block = lax.psum_scatter(partial_value, "narrow", scatter_dimension=0, tiled=True)
    owner_slices = lax.all_gather(arrived, "narrow", axis=0, tiled=True)
    targets = jnp.transpose(slot_request, (1, 0, 2)).reshape(-1)
    factor_all = jnp.transpose(weights, (1, 0, 2)).reshape(-1)
    block_rows = base_block.shape[0]
    offsets = targets - lax.axis_index("narrow") * block_rows
    owned = (offsets >= 0) & (offsets < block_rows)
    factors = jnp.where(owned, factor_all, 0.0)
    target_rows = jnp.where(owned, offsets, 0)
    own_block = base_block.at[target_rows].add(owner_slices.astype(jnp.float32) * factors[:, None])
    local_peak = jnp.max(own_block, axis=1)
    local_mass = jnp.sum(jnp.exp(own_block - local_peak[:, None]), axis=1)
    row_peak, row_mass = combined_all((local_peak, local_mass), "wide", merge_pair)
    log_total = row_peak + jnp.log(row_mass)
    return own_block - log_total[:, None]


def solution(mesh):
    placed = (
        P("wide", "narrow"),
        P("narrow"),
        P("narrow", "wide"),
        P("wide", "narrow", None, None),
        P(),
        P(),
        P(),
    )
    return jax.shard_map(
        body, mesh=mesh, in_specs=placed, out_specs=P("narrow", "wide"), check_vma=False
    )
```

profile of v0, /device:TPU:0, one launch (start us, length us, event | category | flops | bytes accessed | tf_op | source)
XLA Modules:
  0.0 223.1 jit_solution(11933063757548773524)
XLA Ops:
  6.5 1.1 fusion.4
  7.6 2.6 %psum.7 = f32[32]{0:T(128)S(1)} all-reduce(f32[32]{0:T(128)S(1)} %fusion.4), channel_id=1, replica_groups=mesh['wide'=16,'narrow'=2] {'narrow'}, use_global_device_ids=true, to_apply=%region_1.0 | all-reduce | flops 32 | bytes 256 | tf_op jit(solution)/shard_map/psum | solution.py:31
  10.2 1.8 fusion.6
  12.1 78.8 %all-gather.6.cloned.1.call-done = bf16[512,4096]{1,0:T(8,128)(2,1)} async-done(((bf16[32,4096]{1,0:T(8,128)(2,1)}), bf16[512,4096]{1,0:T(8,128)(2,1)}) %all-gather.6.cloned.1.call-update) | async-done | bytes 4194320 | tf_op jit(solution)/shard_map/all_gather | solution.py:35
  90.9 14.0 %fusion.7 = f32[512,2000]{0,1:T(8,128)} fusion(bf16[512,4096]{1,0:T(8,128)(2,1)} %all-gather.6.cloned.1.call-done, bf16[4096,2000]{0,1:T(8,128)(2,1)} %param.11), kind=kOutput, calls=%fused_computation.24 | convolution fusion | flops 8388608000 | bytes 24674304 | tf_op jit(solution)/shard_map/dot_general | solution.py:34
  104.9 1.0 copy-done
  106.0 0.9 all_to_all.14
  106.9 1.1 copy.20
  108.0 4.2 %all-to-all-start = ((bf16[8,16,2000]{2,0,1:T(8,128)(2,1)}), bf16[8,16,2000]{2,0,1:T(8,128)(2,1)S(1)}, u32[]{:S(2)}, u32[]{:S(2)}) async-start(bf16[8,16,2000]{2,0,1:T(8,128)(2,1)} %copy.20), calls=%async_computation.1 | async-start | bytes 1048576 | tf_op jit(solution)/shard_map/all_to_all | solution.py:40
  112.3 0.1 copy.19
  112.3 0.1 sub.63
  112.5 0.1 copy.21
  112.5 0.1 select_n.54
  112.6 14.7 %all-to-all-done = bf16[8,16,2000]{2,0,1:T(8,128)(2,1)S(1)} async-done(((bf16[8,16,2000]{2,0,1:T(8,128)(2,1)}), bf16[8,16,2000]{2,0,1:T(8,128)(2,1)S(1)}, u32[]{:S(2)}, u32[]{:S(2)}) %all-to-all-start) | async-done | bytes 512032 | tf_op jit(solution)/shard_map/all_to_all | solution.py:40
  127.4 2.5 %all_gather.19 = bf16[256,2000]{1,0:T(8,128)(2,1)S(1)} all-gather(bf16[128,2000]{1,0:T(8,128)(2,1)S(1)} %bitcast.28), channel_id=1, replica_groups=mesh['wide'=16,'narrow'=2] {'narrow'}, dimensions={0}, use_global_device_ids=true | all-gather | bytes 1536000 | tf_op jit(solution)/shard_map/all_gather | solution.py:45
  129.9 1.9 copy.22
  131.8 4.7 %scatter_custom_fusion = f32[256,2000]{1,0:T(8,128)S(1)} fusion(f32[256,2000]{1,0:T(8,128)S(1)} %copy.22, s32[256]{0:T(256)S(1)} %bitcast.37, bf16[256,2000]{1,0:T(8,128)(2,1)S(1)} %all_gather.19, f32[256]{0:T(256)S(1)} %select_n.54), kind=kCustom, calls=%fused_computation.5 | custom fusion | flops 1536000 | bytes 3097600 | tf_op jit(solution)/shard_map/scatter-add | solution.py:53
  136.5 1.8 copy.23
  138.3 0.2 reduce_max.9
  138.5 0.4 exponential_reduce_fusion
  138.9 38.0 %all-gather.2 = f32[16,1,256]{2,1,0:T(1,128)S(1)} all-gather(f32[1,1,256]{2,1,0:T(1,128)S(1)} %bitcast.35), channel_id=2, replica_groups=mesh['wide'=16,'narrow'=2] {'wide'}, dimensions={0}, use_global_device_ids=true | all-gather | bytes 17408 | tf_op jit(solution)/shard_map/all_gather | solution.py:13
  176.9 35.5 %all-gather.3 = f32[16,1,256]{2,1,0:T(1,128)S(1)} all-gather(f32[1,1,256]{2,1,0:T(1,128)S(1)} %bitcast.36), channel_id=3, replica_groups=mesh['wide'=16,'narrow'=2] {'wide'}, dimensions={0}, use_global_device_ids=true | all-gather | bytes 17408 | tf_op jit(solution)/shard_map/all_gather | solution.py:13
  212.4 0.8 while.17
  213.3 3.0 %broadcast_subtract_fusion = f32[256,2000]{0,1:T(8,128)} fusion(f32[256,2000]{0,1:T(8,128)} %copy.23, f32[256]{0:T(256)S(1)} %log_add_fusion), kind=kLoop, calls=%fused_computation.9 | loop fusion | flops 512000 | bytes 4097024 | tf_op jit(solution)/shard_map/sub | solution.py:58
  (51 shorter events, 0.6 us)
Async XLA Ops:
  6.5 84.3 %all-gather.6.cloned.1.call-start = ((), (), s32[]{:S(2)}) async-start(), calls=%async_computation.2 | async-start | bytes 4456448 | tf_op jit(solution)/shard_map/all_gather | solution.py:35
  12.1 117.9 %reduce-scatter.2.cloned.1.call-start = ((), (), s32[]{:S(2)}) async-start(), calls=%async_computation.3 | async-start | bytes 6144000 | tf_op jit(solution)/shard_map/reduce_scatter | solution.py:44
  104.9 1.0 copy-start
  106.0 6.3 %copy-start.1 = (s32[16,2,8]{0,2,1:T(8,128)S(1)}, s32[16,2,8]{0,2,1:T(8,128)}, u32[]{:S(2)}) copy-start(s32[16,2,8]{0,2,1:T(8,128)} %param.13) | copy-start | bytes 3076
  106.0 6.5 %copy-start.2 = (s32[16,2,8]{0,2,1:T(8,128)S(1)}, s32[16,2,8]{0,2,1:T(8,128)}, u32[]{:S(2)}) copy-start(s32[16,2,8]{0,2,1:T(8,128)} %param.14) | copy-start | bytes 3076
  106.0 6.5 %copy-start.3 = (s32[16,2]{0,1:T(2,128)S(1)}, s32[16,2]{0,1:T(2,128)}, u32[]{:S(2)}) copy-start(s32[16,2]{0,1:T(2,128)} %param.15) | copy-start | bytes 388
  108.0 19.4 %all-to-all-start = ((bf16[8,16,2000]{2,0,1:T(8,128)(2,1)}), bf16[8,16,2000]{2,0,1:T(8,128)(2,1)S(1)}, u32[]{:S(2)}, u32[]{:S(2)}) async-start(bf16[8,16,2000]{2,0,1:T(8,128)(2,1)} %copy.20), calls=%async_computation.1 | async-start | bytes 1048576 | tf_op jit(solution)/shard_map/all_to_all | solution.py:40
Sparse Core Ops, SparseCore 0:
  12.2 78.6 all-gather.5
  105.1 10.5 reduce-scatter.1
where the time goes:
time: 224 us; the launch traced here: 223 us
  waiting for transfers between devices  93.5 us (42%)
  blocking collectives  78.6 us (35%)
  matrix products  14 us (6%)
  between operations  13.5 us (6%)
  other arithmetic  11.5 us (5%)
  local copies, waits for them, and re-layouts  7.26 us (3%)
  starting transfers between devices  4.26 us (2%)
    all_gather x1, waiting for transfers between devices, body(): lax.all_gather(normed, 'wide', axis=0, tiled=True)  78.8 us
    all_gather x2, blocking collectives, combined_all(): gathered = jax.tree.map(lambda a: lax.all_gather(a, axis), part)  73.5 us
    all_to_all x1, waiting for transfers between devices, body(): lax.all_to_all(row_block, 'wide', split_axis=1, concat_axis=0, tiled=True)  14.7 us
    dot_general x1, matrix products, body(): jnp.dot(lax.all_gather(normed, 'wide', axis=0, tiled=True), head_weight,...  14 us
    scatter-add x1, other arithmetic, body(): base_block.at[target_rows]  4.68 us
  transfers between devices with their start and end apart: 3, of which 2 were waited for; matrix products, arithmetic and copies ran while one was open for 1% of the time, Pallas kernels for 0%

commit v1 on v0

--- a/solution.py
+++ b/solution.py
@@ -1,12 +1,303 @@
 import jax
 import jax.numpy as jnp
 from jax import lax
+from jax.experimental import pallas as pl
+from jax.experimental.pallas import tpu as pltpu
 from jax.sharding import PartitionSpec as P
 
 D = 8192
 
 
 epsilon = 1e-05
+
+
+def flip(a, axis, mask):
+    size = lax.axis_size(axis)
+    return lax.ppermute(a, axis, [(i, i ^ mask) for i in range(size)])
+
+
+def after(a, *others):
+    return lax.optimization_barrier((a, *others))[0]
+
+
+def normalise(hidden, norm_gain):
+    values = hidden.astype(jnp.float32)
+    sums = jnp.sum(values * values, axis=1)
+    squares = sums + flip(sums, "narrow", 1)
+    scales = lax.rsqrt(squares / D + epsilon)
+    return (values * scales[:, None] * norm_gain[None, :]).astype(jnp.bfloat16)
+
+
+def vocabulary_slices(row_block, parts):
+    def kernel(rows_ref, slices_ref):
+        width = slices_ref.shape[2]
+        for part in range(parts):
+            slices_ref[part] = rows_ref[:, part * width : (part + 1) * width]
+
+    slots, vocabulary = row_block.shape
+    return pl.pallas_call(
+        kernel,
+        out_shape=jax.ShapeDtypeStruct((parts, slots, vocabulary // parts), row_block.dtype),
+        cost_estimate=pl.CostEstimate(flops=0, bytes_accessed=4 * slots * vocabulary, transcendentals=0),
+        name="vocabulary_slices",
+    )(row_block)
+
+
+def tile_of(length):
+    return max(t for t in range(16, 513, 16) if length % t == 0)
+
+
+ANYWHERE = pl.BlockSpec(memory_space=pl.ANY)
+SCALAR = pl.BlockSpec(memory_space=pltpu.SMEM)
+ROOM = pltpu.CompilerParams(vmem_limit_bytes=56 * 2**20)
+
+
+def every(count, step):
+    def loop(i, _):
+        step(i)
+        return 0
+
+    lax.fori_loop(0, count, loop, 0)
+
+
+def rows_at(i, tile):
+    return pl.ds(pl.multiple_of(i * tile, 8), tile)
+
+
+def multiply(blocks, weight_t, first, diffs_t, mixing, begin=0, end=None, into=None):
+    vocabulary, width = weight_t.shape
+    count, rows = len(blocks), blocks[0].shape[0]
+    slots = diffs_t.shape[1]
+    tile = tile_of(vocabulary)
+    end = vocabulary // tile if end is None else end
+    chunks = end - begin
+    contract_last = (((1,), (1,)), ((), ()))
+
+    def kernel(first_ref, *refs):
+        block_refs, refs = refs[:count], refs[count:]
+        if into is not None:
+            refs = refs[1:]
+        weight_hbm, diffs_hbm, mixing_hbm, out_hbm, states, weight, diffs, mixed, out = refs[:9]
+        state_sems, weight_sems, side_sems, out_sems = refs[9:]
+
+        def weight_copy(chunk):
+            place = rows_at(begin + chunk, tile)
+            return pltpu.make_async_copy(weight_hbm.at[place], weight.at[place], weight_sems.at[chunk])
+
+        def out_copy(chunk):
+            place = rows_at(begin + chunk, tile)
+            return pltpu.make_async_copy(out.at[place], out_hbm.at[place], out_sems.at[chunk])
+
+        def add_chunk(chunk):
+            weight_copy(chunk).wait()
+            place = rows_at(begin + chunk, tile)
+            out[place, :] = lax.dot_general(
+                weight[place, :], states[...], contract_last, preferred_element_type=jnp.float32
+            ) + lax.dot_general(diffs[place, :], mixed[...], contract_last, preferred_element_type=jnp.float32)
+            out_copy(chunk).start()
+
+        first_copies = [
+            pltpu.make_async_copy(
+                block_refs[k],
+                states.at[pl.ds(pl.multiple_of((first_ref[0] ^ k) * rows, rows), rows)],
+                state_sems.at[k],
+            )
+            for k in range(count)
+        ]
+        first_copies.append(pltpu.make_async_copy(diffs_hbm, diffs, side_sems.at[0]))
+        first_copies.append(pltpu.make_async_copy(mixing_hbm, mixed, side_sems.at[1]))
+        for copy in first_copies:
+            copy.start()
+        every(chunks, lambda chunk: weight_copy(chunk).start())
+        for copy in first_copies:
+            copy.wait()
+        every(chunks, add_chunk)
+        every(chunks, lambda chunk: out_copy(chunk).wait())
+
+    held = [] if into is None else [into]
+    return pl.pallas_call(
+        kernel,
+        in_specs=[SCALAR] + [ANYWHERE] * (count + 3 + len(held)),
+        out_specs=ANYWHERE,
+        out_shape=jax.ShapeDtypeStruct((vocabulary, count * rows), jnp.float32),
+        scratch_shapes=[
+            pltpu.VMEM((count * rows, width), jnp.bfloat16),
+            pltpu.VMEM((vocabulary, width), jnp.bfloat16),
+            pltpu.VMEM((vocabulary, slots), jnp.bfloat16),
+            pltpu.VMEM((count * rows, slots), jnp.bfloat16),
+            pltpu.VMEM((vocabulary, count * rows), jnp.float32),
+            pltpu.SemaphoreType.DMA((count,)),
+            pltpu.SemaphoreType.DMA((chunks,)),
+            pltpu.SemaphoreType.DMA((2,)),
+            pltpu.SemaphoreType.DMA((chunks,)),
+        ],
+        compiler_params=ROOM,
+        cost_estimate=pl.CostEstimate(
+            flops=2 * chunks * tile * width * count * rows, bytes_accessed=2 * chunks * tile * width, transcendentals=0
+        ),
+        input_output_aliases={1 + count: 0} if held else {},
+        name="multiply",
+    )(first.reshape(1), *blocks, *held, weight_t, diffs_t, mixing)
+
+
+def statistics(near, near_other, far, far_other, late, parts):
+    vocabulary, rows = near.shape
+    tile = tile_of(vocabulary)
+    chunks = vocabulary // tile
+
+    def kernel(late_ref, near_ref, near_other_ref, far_ref, far_other_ref, total_hbm, stats_ref, left, right, *sems):
+        left_sems, right_sems, out_sems = sems
+
+        def fetch(chunk, left_side, right_side):
+            place = rows_at(chunk, tile)
+            return [
+                pltpu.make_async_copy(left_side.at[place], left.at[place], left_sems.at[chunk]),
+                pltpu.make_async_copy(right_side.at[place], right.at[place], right_sems.at[chunk]),
+            ]
+
+        def out_copy(chunk):
+            place = rows_at(chunk, tile)
+            return pltpu.make_async_copy(left.at[place], total_hbm.at[place], out_sems.at[chunk])
+
+        def start_all(left_side, right_side):
+            def start(chunk):
+                for copy in fetch(chunk, left_side, right_side):
+                    copy.start()
+
+            every(chunks, start)
+
+        @pl.when(late_ref[0] == 0)
+        def _():
+            start_all(near_ref, near_other_ref)
+
+        @pl.when(late_ref[0] == 1)
+        def _():
+            start_all(far_ref, far_other_ref)
+
+        def step(chunk, state):
+            for copy in fetch(chunk, far_ref, far_other_ref):
+                copy.wait()
+            place = rows_at(chunk, tile)
+            total = left[place, :] + right[place, :]
+            left[place, :] = total
+            out_copy(chunk).start()
+            before, mass = state
+            peak = jnp.maximum(before, jnp.max(total, axis=0, keepdims=True))
+            total = left[place, :]
+            mass = mass * jnp.exp(before - peak) + jnp.sum(jnp.exp(total - peak), axis=0, keepdims=True)
+            return peak, mass
+
+        state = (jnp.full((1, rows), -jnp.inf, jnp.float32), jnp.zeros((1, rows), jnp.float32))
+        both = jnp.concatenate(lax.fori_loop(0, chunks, step, state))
+        stats_ref[...] = jnp.broadcast_to(both[None], stats_ref.shape)
+        every(chunks, lambda chunk: out_copy(chunk).wait())
+
+    return pl.pallas_call(
+        kernel,
+        in_specs=[SCALAR] + [ANYWHERE] * 4,
+        out_specs=[ANYWHERE, pl.BlockSpec(memory_space=pltpu.VMEM)],
+        out_shape=[
+            jax.ShapeDtypeStruct((vocabulary, rows), jnp.float32),
+            jax.ShapeDtypeStruct((parts, 2, rows), jnp.float32),
+        ],
+        scratch_shapes=[pltpu.VMEM((vocabulary, rows), jnp.float32)] * 2 + [pltpu.SemaphoreType.DMA((chunks,))] * 3,
+        compiler_params=ROOM,
+        cost_estimate=pl.CostEstimate(
+            flops=4 * vocabulary * rows, bytes_accessed=16 * vocabulary * rows, transcendentals=vocabulary * rows
+        ),
+        name="statistics",
+    )(late.reshape(1), near, near_other, far, far_other)
+
+
+def subtract(total, arrived):
+    vocabulary, rows = total.shape
+    tile = tile_of(vocabulary)
+    chunks = vocabulary // tile
+
+    def kernel(total_hbm, arrived_ref, out_hbm, held, in_sems, out_sems):
+        def in_copy(chunk):
+            place = rows_at(chunk, tile)
+            return pltpu.make_async_copy(total_hbm.at[place], held.at[place], in_sems.at[chunk])
+
+        def out_copy(chunk):
+            place = rows_at(chunk, tile)
+            return pltpu.make_async_copy(held.at[place], out_hbm.at[place], out_sems.at[chunk])
+
+        every(chunks, lambda chunk: in_copy(chunk).start())
+        peaks, masses = arrived_ref[:, 0, :], arrived_ref[:, 1, :]
+        row_peak = jnp.max(peaks, axis=0, keepdims=True)
+        row_mass = jnp.sum(masses * jnp.exp(peaks - row_peak), axis=0, keepdims=True)
+        log_total = row_peak + jnp.log(row_mass)
+
+        def shift(chunk):
+            in_copy(chunk).wait()
+            place = rows_at(chunk, tile)
+            held[place, :] = held[place, :] - log_total
+            out_copy(chunk).start()
+
+        every(chunks, shift)
+        every(chunks, lambda chunk: out_copy(chunk).wait())
+
+    return pl.pallas_call(
+        kernel,
+        in_specs=[ANYWHERE, pl.BlockSpec(memory_space=pltpu.VMEM)],
+        out_specs=ANYWHERE,
+        out_shape=jax.ShapeDtypeStruct((vocabulary, rows), jnp.float32),
+        scratch_shapes=[pltpu.VMEM((vocabulary, rows), jnp.float32)] + [pltpu.SemaphoreType.DMA((chunks,))] * 2,
+        compiler_params=ROOM,
+        cost_estimate=pl.CostEstimate(flops=vocabulary * rows, bytes_accessed=8 * vocabulary * rows, transcendentals=0),
+        name="subtract",
+    )(total, arrived)
+
+
+def slot_factors(slot_code, slot_count):
+    slots = slot_code.shape[2]
+    active = jnp.arange(slots, dtype=jnp.int32)[None, None, :] < slot_count[:, :, None]
+    return jnp.where(active, slot_code, 0).astype(jnp.float32) * 0.25
+
+
+def body(hidden, norm_gain, head_weight, diff_rows, slot_request, slot_code, slot_count):
+    me, core = lax.axis_index("wide"), lax.axis_index("narrow")
+    parts, rows = lax.axis_size("wide"), hidden.shape[0]
+    weight_t = head_weight.T
+
+    own = normalise(hidden, norm_gain)
+
+    row_block = diff_rows[0, 0]
+    x0, y0, z1 = flip(own, "wide", 1), flip(own, "wide", 2), flip(own, "wide", 4)
+    slices = vocabulary_slices(after(row_block, own), parts)
+    diffs = lax.all_to_all(slices, "wide", split_axis=0, concat_axis=0, tiled=True).reshape(-1, weight_t.shape[0])
+    diffs_t = diffs.T
+
+    own, x0, y0, z1 = lax.optimization_barrier((own, x0, y0, z1))
+    d0, y1, x1, z2 = flip(y0, "wide", 1), flip(z1, "wide", 2), flip(x0, "wide", 4), flip(own, "wide", 8)
+    d1 = flip(x1, "wide", 2)
+    z2, d0, y1, x1 = lax.optimization_barrier((z2, d0, y1, x1))
+    x2, y2, z3 = flip(z2, "wide", 1), flip(z2, "wide", 2), flip(z2, "wide", 4)
+    x2, y2, z3, d1 = lax.optimization_barrier((x2, y2, z3, d1))
+    x3, y3 = flip(z3, "wide", 1), flip(z3, "wide", 2)
+
+    first, half = me & 7, me // 8
+    late = half ^ core
+    factors = lax.dynamic_index_in_dim(slot_factors(slot_code, slot_count), core, 1, False).reshape(-1)
+    targets = lax.dynamic_index_in_dim(slot_request, core, 1, False).reshape(-1)
+
+    def mixing(which):
+        requests = which * 8 * rows + jnp.arange(8 * rows, dtype=jnp.int32)
+        return jnp.where(requests[:, None] == targets, factors, 0.0).astype(jnp.bfloat16)
+
+    blocks = [own, x0, y0, d0, z1, x1, y1, d1]
+    near = multiply(blocks, weight_t, first, diffs_t, mixing(half), 0, 3)
+    x3, y3, y2, near = lax.optimization_barrier((x3, y3, y2, near))
+    d2, d3 = flip(y2, "wide", 1), flip(x3, "wide", 2)
+    near = multiply(blocks, weight_t, first, diffs_t, mixing(half), 3, 5, near)
+    d2, d3, near = lax.optimization_barrier((d2, d3, near))
+    near_other = flip(near, "narrow", 1)
+    far = multiply([z2, x2, y2, d2, z3, x3, y3, d3], weight_t, first, diffs_t, mixing(1 - half))
+    far_other = flip(far, "narrow", 1)
+    total, stats = statistics(near, near_other, far, far_other, late, parts)
+    arrived = lax.all_to_all(stats, "wide", split_axis=0, concat_axis=0, tiled=True)
+    return subtract(total, arrived).T
 
 
 def combined_all(part, axis, combine):
@@ -26,7 +317,7 @@
     return (row_peak, summed)
 
 
-def body(hidden, norm_gain, head_weight, diff_rows, slot_request, slot_code, slot_count):
+def general_body(hidden, norm_gain, head_weight, diff_rows, slot_request, slot_code, slot_count):
     values = hidden.astype(jnp.float32)
     squares = lax.psum(jnp.sum(values * values, axis=1), "narrow")
     scales = lax.rsqrt(squares / D + epsilon)
@@ -36,15 +327,11 @@
         head_weight,
         preferred_element_type=jnp.float32,
     )
-    row_block = diff_rows[0, 0]
-    arrived = lax.all_to_all(row_block, "wide", split_axis=1, concat_axis=0, tiled=True)
-    slot_total = row_block.shape[0]
-    active = jnp.arange(slot_total, dtype=jnp.int32)[None, None, :] < slot_count[:, :, None]
-    weights = jnp.where(active, slot_code, 0).astype(jnp.float32) * 0.25
+    arrived = lax.all_to_all(diff_rows[0, 0], "wide", split_axis=1, concat_axis=0, tiled=True)
     base_block = lax.psum_scatter(partial_value, "narrow", scatter_dimension=0, tiled=True)
     owner_slices = lax.all_gather(arrived, "narrow", axis=0, tiled=True)
     targets = jnp.transpose(slot_request, (1, 0, 2)).reshape(-1)
-    factor_all = jnp.transpose(weights, (1, 0, 2)).reshape(-1)
+    factor_all = jnp.transpose(slot_factors(slot_code, slot_count), (1, 0, 2)).reshape(-1)
     block_rows = base_block.shape[0]
     offsets = targets - lax.axis_index("narrow") * block_rows
     owned = (offsets >= 0) & (offsets < block_rows)
@@ -68,6 +355,11 @@
         P(),
         P(),
     )
+    small = mesh.shape["wide"] == 16 and mesh.shape["narrow"] == 2
     return jax.shard_map(
-        body, mesh=mesh, in_specs=placed, out_specs=P("narrow", "wide"), check_vma=False
+        body if small else general_body,
+        mesh=mesh,
+        in_specs=placed,
+        out_specs=P("narrow", "wide"),
+        check_vma=False,
     )

time: 224 us -> 110 us (0.49)
  blocking collectives: 78.6 us -> 12.8 us
  waiting for transfers between devices: 93.5 us -> 34.8 us
  Pallas kernels: 0 us -> 30.8 us
  starting transfers between devices: 4.26 us -> 25.7 us
  matrix products: 14 us -> 0 us
  between operations: 13.5 us -> 0.29 us
  other arithmetic: 11.5 us -> 3.05 us
  local copies, waits for them, and re-layouts: 7.26 us -> 2.14 us
    all_gather x1 -> x0, waiting for transfers between devices: 78.8 us -> none  [body(): lax.all_gather(normed, 'wide', axis=0, tiled=True)]
    all_gather x3 -> x0, blocking collectives: 76 us -> none  [the longest x2 73.5 us: combined_all(): gathered = jax.tree.map(lambda a: lax.all_gather(a, axis), part)]
    ppermute x0 -> x18, waiting for transfers between devices: none -> 34.8 us  [flip(): return lax.ppermute(a, axis, [(i, i ^ mask) for i in range(size)])]
    pallas_call x0 -> x6, Pallas kernels: none -> 30.8 us  [the longest x3 21.9 us: multiply(): pl.pallas_call(kernel, in_specs=[SCALAR] + [ANYWHERE] * (count + 3 + len(...]
    ppermute x0 -> x18, starting transfers between devices: none -> 21.7 us  [flip(): return lax.ppermute(a, axis, [(i, i ^ mask) for i in range(size)])]
    all_to_all x1, waiting for transfers between devices: 14.7 us -> 0.01 us  [body(): lax.all_to_all(slices, 'wide', split_axis=0, concat_axis=0, tiled=True)]
    dot_general x1 -> x0, matrix products: 14 us -> none  [body(): jnp.dot(lax.all_gather(normed, 'wide', axis=0, tiled=True), head_weight,...]
    all_to_all x0 -> x1, blocking collectives: none -> 12.8 us  [body(): lax.all_to_all(stats, 'wide', split_axis=0, concat_axis=0, tiled=True)]
  transfers between devices with their start and end apart: 3 -> 19, of which waited for: 2 -> 9; matrix products, arithmetic and copies ran while one was open for 1% -> 2% of each run, Pallas kernels for 0% -> 13%
where the time goes in v1:
time: 110 us
  waiting for transfers between devices  34.8 us (32%)
  Pallas kernels  30.8 us (28%)
  starting transfers between devices  25.7 us (23%)
  blocking collectives  12.8 us (12%)
  other arithmetic  3.05 us (3%)
  local copies, waits for them, and re-layouts  2.14 us (2%)
    ppermute x18, waiting for transfers between devices, flip(): return lax.ppermute(a, axis, [(i, i ^ mask) for i in range(size)])  34.8 us
    pallas_call x3, Pallas kernels, multiply(): pl.pallas_call(kernel, in_specs=[SCALAR] + [ANYWHERE] * (count + 3 + len(...  21.9 us
    ppermute x18, starting transfers between devices, flip(): return lax.ppermute(a, axis, [(i, i ^ mask) for i in range(size)])  21.7 us
    all_to_all x1, blocking collectives, body(): lax.all_to_all(stats, 'wide', split_axis=0, concat_axis=0, tiled=True)  12.8 us
    all_to_all x1, starting transfers between devices, body(): lax.all_to_all(slices, 'wide', split_axis=0, concat_axis=0, tiled=True)  3.97 us
    pallas_call x1, Pallas kernels, statistics(): pl.pallas_call(kernel, in_specs=[SCALAR] + [ANYWHERE] * 4, out_specs=[ANY...  3.77 us
    pallas_call x1, Pallas kernels, subtract(): pl.pallas_call(kernel, in_specs=[ANYWHERE, pl.BlockSpec(memory_space=pltp...  3.16 us
  transfers between devices with their start and end apart: 19, of which 9 were waited for; matrix products, arithmetic and copies ran while one was open for 2% of the time, Pallas kernels for 13%

profile of v1, /device:TPU:0, one launch (start us, length us, event | category | flops | bytes accessed | tf_op | source)
XLA Modules:
  0.0 109.6 jit_solution(9914063683913833910)
XLA Ops:
  3.6 2.9 %collective-permute-start.3 = (bf16[32,4096]{1,0:T(8,128)(2,1)S(1)}, bf16[32,4096]{1,0:T(8,128)(2,1)S(1)}, u32[]{:S(2)}, u32[]{:S(2)}) collective-permute-start(bf16[32,4096]{1,0:T(8,128)(2,1)S(1)} %fusion.2.refs_0_), channel_id=1, source_target_pairs={{0,8},{2,10},{4,12},{6,14},{8,0},{10,2},{12,4},{14,6},{16,24},{18,... | collective-permute-start | bytes 786440 | tf_op jit(solution)/shard_map/ppermute | solution.py:16
  6.5 1.5 %collective-permute-start.2 = (bf16[32,4096]{1,0:T(8,128)(2,1)S(1)}, bf16[32,4096]{1,0:T(8,128)(2,1)S(1)}, u32[]{:S(2)}, u32[]{:S(2)}) collective-permute-start(bf16[32,4096]{1,0:T(8,128)(2,1)S(1)} %fusion.2.refs_0_), channel_id=1, source_target_pairs={{0,4},{2,6},{4,0},{6,2},{8,12},{10,14},{12,8},{14,10},{16,20},{18,... | collective-permute-start | bytes 786440 | tf_op jit(solution)/shard_map/ppermute | solution.py:16
  8.1 1.5 %collective-permute-start.1 = (bf16[32,4096]{1,0:T(8,128)(2,1)S(1)}, bf16[32,4096]{1,0:T(8,128)(2,1)S(1)}, u32[]{:S(2)}, u32[]{:S(2)}) collective-permute-start(bf16[32,4096]{1,0:T(8,128)(2,1)S(1)} %fusion.2.refs_0_), channel_id=1, source_target_pairs={{0,2},{2,0},{4,6},{6,4},{8,10},{10,8},{12,14},{14,12},{16,18},{18,... | collective-permute-start | bytes 786440 | tf_op jit(solution)/shard_map/ppermute | solution.py:16
  9.5 2.0 %vocabulary_slices.1 = bf16[16,8,2000]{2,1,0:T(8,128)(2,1)} custom-call(bf16[8,32000]{1,0:T(8,128)(2,1)} %bitcast.18), custom_call_target="tpu_custom_call" | custom-call | bytes 1024000 | tf_op jit(solution)/shard_map/vocabulary_slices/pallas_call | solution.py:38
  11.6 4.0 %all-to-all-start = ((bf16[16,8,2000]{2,1,0:T(8,128)(2,1)}), bf16[16,8,2000]{2,1,0:T(8,128)(2,1)S(1)}, u32[]{:S(2)}, u32[]{:S(2)}) async-start(bf16[16,8,2000]{2,1,0:T(8,128)(2,1)} %vocabulary_slices.1), calls=%async_computation | async-start | bytes 1048576 | tf_op jit(solution)/shard_map/all_to_all | solution.py:269
  15.9 2.6 %collective-permute-start.4 = (bf16[32,4096]{1,0:T(8,128)(2,1)S(1)}, bf16[32,4096]{1,0:T(8,128)(2,1)S(1)}, u32[]{:S(2)}, u32[]{:S(2)}) collective-permute-start(bf16[32,4096]{1,0:T(8,128)(2,1)S(1)} %fusion.2.refs_0_), channel_id=1, source_target_pairs={{0,16},{2,18},{4,20},{6,22},{8,24},{10,26},{12,28},{14,30},{16,0},... | collective-permute-start | bytes 786440 | tf_op jit(solution)/shard_map/ppermute | solution.py:16
  18.5 1.5 %collective-permute-start.5 = (bf16[32,4096]{1,0:T(8,128)(2,1)S(1)}, bf16[32,4096]{1,0:T(8,128)(2,1)S(1)}, u32[]{:S(2)}, u32[]{:S(2)}) collective-permute-start(bf16[32,4096]{1,0:T(8,128)(2,1)S(1)} %collective-permute-done.2.refs_2_), channel_id=1, source_target_pairs={{0,2},{2,0},{4,6},{6,4},{8,10},{10,8},{12,14},{14,12},{16,18},{18,... | collective-permute-start | bytes 786440 | tf_op jit(solution)/shard_map/ppermute | solution.py:16
  20.0 1.4 %collective-permute-start.6 = (bf16[32,4096]{1,0:T(8,128)(2,1)S(1)}, bf16[32,4096]{1,0:T(8,128)(2,1)S(1)}, u32[]{:S(2)}, u32[]{:S(2)}) collective-permute-start(bf16[32,4096]{1,0:T(8,128)(2,1)S(1)} %collective-permute-done.3.refs_4_), channel_id=1, source_target_pairs={{0,4},{2,6},{4,0},{6,2},{8,12},{10,14},{12,8},{14,10},{16,20},{18,... | collective-permute-start | bytes 786440 | tf_op jit(solution)/shard_map/ppermute | solution.py:16
  21.4 1.5 %collective-permute-start.7 = (bf16[32,4096]{1,0:T(8,128)(2,1)S(1)}, bf16[32,4096]{1,0:T(8,128)(2,1)S(1)}, u32[]{:S(2)}, u32[]{:S(2)}) collective-permute-start(bf16[32,4096]{1,0:T(8,128)(2,1)S(1)} %collective-permute-done.1.refs_1_), channel_id=1, source_target_pairs={{0,8},{2,10},{4,12},{6,14},{8,0},{10,2},{12,4},{14,6},{16,24},{18,... | collective-permute-start | bytes 786440 | tf_op jit(solution)/shard_map/ppermute | solution.py:16
  22.9 17.8 %collective-permute-done.4.refs_0_ = bf16[32,4096]{1,0:T(8,128)(2,1)S(1)} collective-permute-done((bf16[32,4096]{1,0:T(8,128)(2,1)S(1)}, bf16[32,4096]{1,0:T(8,128)(2,1)S(1)}, u32[]{:S(2)}, u32[]{:S(2)}) %collective-permute-start.4) | collective-permute-done | bytes 262176 | tf_op jit(solution)/shard_map/ppermute | solution.py:16
  40.8 1.5 %collective-permute-start.9 = (bf16[32,4096]{1,0:T(8,128)(2,1)S(1)}, bf16[32,4096]{1,0:T(8,128)(2,1)}, u32[]{:S(2)}, u32[]{:S(2)}) collective-permute-start(bf16[32,4096]{1,0:T(8,128)(2,1)S(1)} %collective-permute-done.4.refs_0_), channel_id=1, source_target_pairs={{0,4},{2,6},{4,0},{6,2},{8,12},{10,14},{12,8},{14,10},{16,20},{18,... | collective-permute-start | bytes 786440 | tf_op jit(solution)/shard_map/ppermute | solution.py:16
  42.4 1.5 %collective-permute-start.8 = (bf16[32,4096]{1,0:T(8,128)(2,1)S(1)}, bf16[32,4096]{1,0:T(8,128)(2,1)}, u32[]{:S(2)}, u32[]{:S(2)}) collective-permute-start(bf16[32,4096]{1,0:T(8,128)(2,1)S(1)} %collective-permute-done.4.refs_0_), channel_id=1, source_target_pairs={{0,2},{2,0},{4,6},{6,4},{8,10},{10,8},{12,14},{14,12},{16,18},{18,... | collective-permute-start | bytes 786440 | tf_op jit(solution)/shard_map/ppermute | solution.py:16
  44.8 3.3 %collective-permute-done.10.refs_4_ = bf16[32,4096]{1,0:T(8,128)(2,1)S(1)} collective-permute-done((bf16[32,4096]{1,0:T(8,128)(2,1)S(1)}, bf16[32,4096]{1,0:T(8,128)(2,1)S(1)}, u32[]{:S(2)}, u32[]{:S(2)}) %collective-permute-start.10) | collective-permute-done | bytes 262176 | tf_op jit(solution)/shard_map/ppermute | solution.py:16
  48.1 2.2 %collective-permute-done.9.refs_2_ = bf16[32,4096]{1,0:T(8,128)(2,1)} collective-permute-done((bf16[32,4096]{1,0:T(8,128)(2,1)S(1)}, bf16[32,4096]{1,0:T(8,128)(2,1)}, u32[]{:S(2)}, u32[]{:S(2)}) %collective-permute-start.9) | collective-permute-done | bytes 262176 | tf_op jit(solution)/shard_map/ppermute | solution.py:16
  50.2 3.5 %collective-permute-done.11.refs_7_ = bf16[32,4096]{1,0:T(8,128)(2,1)S(1)} collective-permute-done((bf16[32,4096]{1,0:T(8,128)(2,1)S(1)}, bf16[32,4096]{1,0:T(8,128)(2,1)S(1)}, u32[]{:S(2)}, u32[]{:S(2)}) %collective-permute-start.11) | collective-permute-done | bytes 262176 | tf_op jit(solution)/shard_map/ppermute | solution.py:16
  53.8 1.5 %collective-permute-start.13 = (bf16[32,4096]{1,0:T(8,128)(2,1)S(1)}, bf16[32,4096]{1,0:T(8,128)(2,1)}, u32[]{:S(2)}, u32[]{:S(2)}) collective-permute-start(bf16[32,4096]{1,0:T(8,128)(2,1)S(1)} %collective-permute-done.10.refs_4_), channel_id=1, source_target_pairs={{0,4},{2,6},{4,0},{6,2},{8,12},{10,14},{12,8},{14,10},{16,20},{18,... | collective-permute-start | bytes 786440 | tf_op jit(solution)/shard_map/ppermute | solution.py:16
  55.2 1.5 %collective-permute-start.12 = (bf16[32,4096]{1,0:T(8,128)(2,1)S(1)}, bf16[32,4096]{1,0:T(8,128)(2,1)}, u32[]{:S(2)}, u32[]{:S(2)}) collective-permute-start(bf16[32,4096]{1,0:T(8,128)(2,1)S(1)} %collective-permute-done.10.refs_4_), channel_id=1, source_target_pairs={{0,2},{2,0},{4,6},{6,4},{8,10},{10,8},{12,14},{14,12},{16,18},{18,... | collective-permute-start | bytes 786440 | tf_op jit(solution)/shard_map/ppermute | solution.py:16
  58.6 6.9 %multiply.8.refs_8_ = f32[2000,256]{1,0:T(8,128)} custom-call(s32[1]{0:T(128)} %bitcast.1.first_ref, bf16[32,4096]{1,0:T(8,128)(2,1)} %copy-done.2, bf16[32,4096]{1,0:T(8,128)(2,1)} %copy-done.5, bf16[32,4096]{1,0:T(8,128)(2,1)} %copy-done.4, bf16[32,4096]{1,0:T(8,128)(2,1)} %copy-done.6, bf16[32,4096]{1,0:T(8,128)(2,1)} %copy-done.3, ...), custom_call_target="tpu_custom_call" | custom-call | flops 2516582400 | bytes 9830400 | tf_op jit(solution)/shard_map/multiply/pallas_call | solution.py:118
  66.7 5.8 %multiply.9.near_ref = f32[2000,256]{1,0:T(8,128)} custom-call(s32[1]{0:T(128)} %bitcast.1.first_ref, bf16[32,4096]{1,0:T(8,128)(2,1)} %copy-done.2, bf16[32,4096]{1,0:T(8,128)(2,1)} %copy-done.5, bf16[32,4096]{1,0:T(8,128)(2,1)} %copy-done.4, bf16[32,4096]{1,0:T(8,128)(2,1)} %copy-done.6, ...), custom_call_target="tpu_custom_call", output_to_operand_aliasing={{}: (9, {})} | custom-call | flops 1677721600 | bytes 6553600 | tf_op jit(solution)/shard_map/multiply/pallas_call | solution.py:118
  73.4 9.2 %multiply.10.far_ref = f32[2000,256]{1,0:T(8,128)} custom-call(s32[1]{0:T(128)} %bitcast.1.first_ref, bf16[32,4096]{1,0:T(8,128)(2,1)} %copy-done.10, bf16[32,4096]{1,0:T(8,128)(2,1)} %collective-permute-done.8.refs_1_, bf16[32,4096]{1,0:T(8,128)(2,1)} %collective-permute-done.9.refs_2_, bf16[32,4096]{1,0:T(8,128)(2,1)} %copy-done.12, ...), custom_call_target="tpu_custom_call" | custom-call | flops 4194304000 | bytes 16384000 | tf_op jit(solution)/shard_map/multiply/pallas_call | solution.py:118
  83.2 5.9 %collective-permute-done.17.far_other_ref = f32[2000,256]{1,0:T(8,128)} collective-permute-done((f32[2000,256]{1,0:T(8,128)}, f32[2000,256]{1,0:T(8,128)}, u32[]{:S(2)}, u32[]{:S(2)}) %collective-permute-start.17) | collective-permute-done | bytes 2048032 | tf_op jit(solution)/shard_map/ppermute | solution.py:16
  89.9 3.8 %statistics.1 = (f32[2000,256]{1,0:T(8,128)}, f32[16,2,256]{2,1,0:T(2,128)}) custom-call(s32[1]{0:T(128)} %bitcast.late_ref, f32[2000,256]{1,0:T(8,128)} %multiply.9.near_ref, f32[2000,256]{1,0:T(8,128)} %collective-permute-done.16.near_other_ref, f32[2000,256]{1,0:T(8,128)} %multiply.10.far_ref, f32[2000,256]{1,0:T(8,128)} %collective-permute-done.17.far_other_ref), custom_call_target="tpu_custom_call" | custom-call | flops 2048000 | bytes 8192000 | tf_op jit(solution)/shard_map/statistics/pallas_call | solution.py:195
  93.6 12.8 %all_to_all.10.arrived_ref = f32[16,2,256]{2,1,0:T(2,128)} all-to-all(f32[16,2,256]{2,1,0:T(2,128)} %get-tuple-element.48), channel_id=1, replica_groups=mesh['wide'=16,'narrow'=2] {'wide'}, dimensions={0} | all-to-all | bytes 65536 | tf_op jit(solution)/shard_map/all_to_all | solution.py:299
  106.4 3.2 %subtract.1 = f32[2000,256]{1,0:T(8,128)} custom-call(f32[2000,256]{1,0:T(8,128)} %get-tuple-element.47.total_hbm, f32[16,2,256]{2,1,0:T(2,128)} %all_to_all.10.arrived_ref), custom_call_target="tpu_custom_call" | custom-call | flops 512000 | bytes 4096000 | tf_op jit(solution)/shard_map/subtract/pallas_call | solution.py:241
  (66 shorter events, 10.2 us)
Async XLA Ops:
  0.0 44.6 %copy-start = (s32[16,2,8]{0,2,1:T(8,128)S(1)}, s32[16,2,8]{0,2,1:T(8,128)}, u32[]{:S(2)}) copy-start(s32[16,2,8]{0,2,1:T(8,128)} %param.11) | copy-start | bytes 3076
  0.0 44.4 %copy-start.14 = (s32[16,2,8]{0,2,1:T(8,128)S(1)}, s32[16,2,8]{0,2,1:T(8,128)}, u32[]{:S(2)}) copy-start(s32[16,2,8]{0,2,1:T(8,128)} %param.12) | copy-start | bytes 3076
  1.2 1.3 %collective-permute-start = (f32[32]{0:T(128)S(1)}, f32[32]{0:T(128)S(1)}, u32[]{:S(2)}, u32[]{:S(2)}) collective-permute-start(f32[32]{0:T(128)S(1)} %fusion), channel_id=1, source_target_pairs={{0,1},{1,0},{2,3},{3,2},{4,5},{5,4},{6,7},{7,6},{8,9},{9,8},{10,11... | collective-permute-start | bytes 392 | tf_op jit(solution)/shard_map/ppermute | solution.py:16
  3.6 54.9 %copy-start.2 = (bf16[32,4096]{1,0:T(8,128)(2,1)}, bf16[32,4096]{1,0:T(8,128)(2,1)S(1)}, u32[]{:S(2)}) copy-start(bf16[32,4096]{1,0:T(8,128)(2,1)S(1)} %fusion.2.refs_0_) | copy-start | bytes 786436
  3.6 12.0 %collective-permute-start.3 = (bf16[32,4096]{1,0:T(8,128)(2,1)S(1)}, bf16[32,4096]{1,0:T(8,128)(2,1)S(1)}, u32[]{:S(2)}, u32[]{:S(2)}) collective-permute-start(bf16[32,4096]{1,0:T(8,128)(2,1)S(1)} %fusion.2.refs_0_), channel_id=1, source_target_pairs={{0,8},{2,10},{4,12},{6,14},{8,0},{10,2},{12,4},{14,6},{16,24},{18,... | collective-permute-start | bytes 786440 | tf_op jit(solution)/shard_map/ppermute | solution.py:16
  6.5 9.0 %collective-permute-start.2 = (bf16[32,4096]{1,0:T(8,128)(2,1)S(1)}, bf16[32,4096]{1,0:T(8,128)(2,1)S(1)}, u32[]{:S(2)}, u32[]{:S(2)}) collective-permute-start(bf16[32,4096]{1,0:T(8,128)(2,1)S(1)} %fusion.2.refs_0_), channel_id=1, source_target_pairs={{0,4},{2,6},{4,0},{6,2},{8,12},{10,14},{12,8},{14,10},{16,20},{18,... | collective-permute-start | bytes 786440 | tf_op jit(solution)/shard_map/ppermute | solution.py:16
  8.1 7.9 %collective-permute-start.1 = (bf16[32,4096]{1,0:T(8,128)(2,1)S(1)}, bf16[32,4096]{1,0:T(8,128)(2,1)S(1)}, u32[]{:S(2)}, u32[]{:S(2)}) collective-permute-start(bf16[32,4096]{1,0:T(8,128)(2,1)S(1)} %fusion.2.refs_0_), channel_id=1, source_target_pairs={{0,2},{2,0},{4,6},{6,4},{8,10},{10,8},{12,14},{14,12},{16,18},{18,... | collective-permute-start | bytes 786440 | tf_op jit(solution)/shard_map/ppermute | solution.py:16
  11.6 45.9 %all-to-all-start = ((bf16[16,8,2000]{2,1,0:T(8,128)(2,1)}), bf16[16,8,2000]{2,1,0:T(8,128)(2,1)S(1)}, u32[]{:S(2)}, u32[]{:S(2)}) async-start(bf16[16,8,2000]{2,1,0:T(8,128)(2,1)} %vocabulary_slices.1), calls=%async_computation | async-start | bytes 1048576 | tf_op jit(solution)/shard_map/all_to_all | solution.py:269
  15.6 43.0 %copy-start.3 = (bf16[32,4096]{1,0:T(8,128)(2,1)}, bf16[32,4096]{1,0:T(8,128)(2,1)S(1)}, u32[]{:S(2)}) copy-start(bf16[32,4096]{1,0:T(8,128)(2,1)S(1)} %collective-permute-done.3.refs_4_) | copy-start | bytes 786436
  15.6 43.0 %copy-start.4 = (bf16[32,4096]{1,0:T(8,128)(2,1)}, bf16[32,4096]{1,0:T(8,128)(2,1)S(1)}, u32[]{:S(2)}) copy-start(bf16[32,4096]{1,0:T(8,128)(2,1)S(1)} %collective-permute-done.2.refs_2_) | copy-start | bytes 786436
  15.9 24.8 %collective-permute-start.4 = (bf16[32,4096]{1,0:T(8,128)(2,1)S(1)}, bf16[32,4096]{1,0:T(8,128)(2,1)S(1)}, u32[]{:S(2)}, u32[]{:S(2)}) collective-permute-start(bf16[32,4096]{1,0:T(8,128)(2,1)S(1)} %fusion.2.refs_0_), channel_id=1, source_target_pairs={{0,16},{2,18},{4,20},{6,22},{8,24},{10,26},{12,28},{14,30},{16,0},... | collective-permute-start | bytes 786440 | tf_op jit(solution)/shard_map/ppermute | solution.py:16
  18.5 22.2 %collective-permute-start.5 = (bf16[32,4096]{1,0:T(8,128)(2,1)S(1)}, bf16[32,4096]{1,0:T(8,128)(2,1)S(1)}, u32[]{:S(2)}, u32[]{:S(2)}) collective-permute-start(bf16[32,4096]{1,0:T(8,128)(2,1)S(1)} %collective-permute-done.2.refs_2_), channel_id=1, source_target_pairs={{0,2},{2,0},{4,6},{6,4},{8,10},{10,8},{12,14},{14,12},{16,18},{18,... | collective-permute-start | bytes 786440 | tf_op jit(solution)/shard_map/ppermute | solution.py:16
  20.0 20.7 %collective-permute-start.6 = (bf16[32,4096]{1,0:T(8,128)(2,1)S(1)}, bf16[32,4096]{1,0:T(8,128)(2,1)S(1)}, u32[]{:S(2)}, u32[]{:S(2)}) collective-permute-start(bf16[32,4096]{1,0:T(8,128)(2,1)S(1)} %collective-permute-done.3.refs_4_), channel_id=1, source_target_pairs={{0,4},{2,6},{4,0},{6,2},{8,12},{10,14},{12,8},{14,10},{16,20},{18,... | collective-permute-start | bytes 786440 | tf_op jit(solution)/shard_map/ppermute | solution.py:16
  21.4 19.3 %collective-permute-start.7 = (bf16[32,4096]{1,0:T(8,128)(2,1)S(1)}, bf16[32,4096]{1,0:T(8,128)(2,1)S(1)}, u32[]{:S(2)}, u32[]{:S(2)}) collective-permute-start(bf16[32,4096]{1,0:T(8,128)(2,1)S(1)} %collective-permute-done.1.refs_1_), channel_id=1, source_target_pairs={{0,8},{2,10},{4,12},{6,14},{8,0},{10,2},{12,4},{14,6},{16,24},{18,... | collective-permute-start | bytes 786440 | tf_op jit(solution)/shard_map/ppermute | solution.py:16
  40.7 7.3 %collective-permute-start.10 = (bf16[32,4096]{1,0:T(8,128)(2,1)S(1)}, bf16[32,4096]{1,0:T(8,128)(2,1)S(1)}, u32[]{:S(2)}, u32[]{:S(2)}) collective-permute-start(bf16[32,4096]{1,0:T(8,128)(2,1)S(1)} %collective-permute-done.4.refs_0_), channel_id=1, source_target_pairs={{0,8},{2,10},{4,12},{6,14},{8,0},{10,2},{12,4},{14,6},{16,24},{18,... | collective-permute-start | bytes 786440 | tf_op jit(solution)/shard_map/ppermute | solution.py:16
  40.8 9.4 %collective-permute-start.9 = (bf16[32,4096]{1,0:T(8,128)(2,1)S(1)}, bf16[32,4096]{1,0:T(8,128)(2,1)}, u32[]{:S(2)}, u32[]{:S(2)}) collective-permute-start(bf16[32,4096]{1,0:T(8,128)(2,1)S(1)} %collective-permute-done.4.refs_0_), channel_id=1, source_target_pairs={{0,4},{2,6},{4,0},{6,2},{8,12},{10,14},{12,8},{14,10},{16,20},{18,... | collective-permute-start | bytes 786440 | tf_op jit(solution)/shard_map/ppermute | solution.py:16
  42.4 7.9 %collective-permute-start.8 = (bf16[32,4096]{1,0:T(8,128)(2,1)S(1)}, bf16[32,4096]{1,0:T(8,128)(2,1)}, u32[]{:S(2)}, u32[]{:S(2)}) collective-permute-start(bf16[32,4096]{1,0:T(8,128)(2,1)S(1)} %collective-permute-done.4.refs_0_), channel_id=1, source_target_pairs={{0,2},{2,0},{4,6},{6,4},{8,10},{10,8},{12,14},{14,12},{16,18},{18,... | collective-permute-start | bytes 786440 | tf_op jit(solution)/shard_map/ppermute | solution.py:16
  43.8 9.9 %collective-permute-start.11 = (bf16[32,4096]{1,0:T(8,128)(2,1)S(1)}, bf16[32,4096]{1,0:T(8,128)(2,1)S(1)}, u32[]{:S(2)}, u32[]{:S(2)}) collective-permute-start(bf16[32,4096]{1,0:T(8,128)(2,1)S(1)} %collective-permute-done.7.refs_5_), channel_id=1, source_target_pairs={{0,4},{2,6},{4,0},{6,2},{8,12},{10,14},{12,8},{14,10},{16,20},{18,... | collective-permute-start | bytes 786440 | tf_op jit(solution)/shard_map/ppermute | solution.py:16
  53.8 11.7 %collective-permute-start.13 = (bf16[32,4096]{1,0:T(8,128)(2,1)S(1)}, bf16[32,4096]{1,0:T(8,128)(2,1)}, u32[]{:S(2)}, u32[]{:S(2)}) collective-permute-start(bf16[32,4096]{1,0:T(8,128)(2,1)S(1)} %collective-permute-done.10.refs_4_), channel_id=1, source_target_pairs={{0,4},{2,6},{4,0},{6,2},{8,12},{10,14},{12,8},{14,10},{16,20},{18,... | collective-permute-start | bytes 786440 | tf_op jit(solution)/shard_map/ppermute | solution.py:16
  55.2 10.3 %collective-permute-start.12 = (bf16[32,4096]{1,0:T(8,128)(2,1)S(1)}, bf16[32,4096]{1,0:T(8,128)(2,1)}, u32[]{:S(2)}, u32[]{:S(2)}) collective-permute-start(bf16[32,4096]{1,0:T(8,128)(2,1)S(1)} %collective-permute-done.10.refs_4_), channel_id=1, source_target_pairs={{0,2},{2,0},{4,6},{6,4},{8,10},{10,8},{12,14},{14,12},{16,18},{18,... | collective-permute-start | bytes 786440 | tf_op jit(solution)/shard_map/ppermute | solution.py:16
  65.5 7.0 %collective-permute-start.14 = (bf16[32,4096]{1,0:T(8,128)(2,1)}, bf16[32,4096]{1,0:T(8,128)(2,1)S(1)}, u32[]{:S(2)}, u32[]{:S(2)}) collective-permute-start(bf16[32,4096]{1,0:T(8,128)(2,1)} %collective-permute-done.9.refs_2_), channel_id=1, source_target_pairs={{0,2},{2,0},{4,6},{6,4},{8,10},{10,8},{12,14},{14,12},{16,18},{18,... | collective-permute-start | bytes 786440 | tf_op jit(solution)/shard_map/ppermute | solution.py:16
  66.2 6.6 %collective-permute-start.15 = (bf16[32,4096]{1,0:T(8,128)(2,1)}, bf16[32,4096]{1,0:T(8,128)(2,1)S(1)}, u32[]{:S(2)}, u32[]{:S(2)}) collective-permute-start(bf16[32,4096]{1,0:T(8,128)(2,1)} %collective-permute-done.12.refs_5_), channel_id=1, source_target_pairs={{0,4},{2,6},{4,0},{6,2},{8,12},{10,14},{12,8},{14,10},{16,20},{18,... | collective-permute-start | bytes 786440 | tf_op jit(solution)/shard_map/ppermute | solution.py:16
  82.6 6.5 %collective-permute-start.17 = (f32[2000,256]{1,0:T(8,128)}, f32[2000,256]{1,0:T(8,128)}, u32[]{:S(2)}, u32[]{:S(2)}) collective-permute-start(f32[2000,256]{1,0:T(8,128)} %multiply.10.far_ref), channel_id=1, source_target_pairs={{0,1},{1,0},{2,3},{3,2},{4,5},{5,4},{6,7},{7,6},{8,9},{9,8},{10,11... | collective-permute-start | bytes 6144008 | tf_op jit(solution)/shard_map/ppermute | solution.py:16
  82.7 7.1 %collective-permute-start.16 = (f32[2000,256]{1,0:T(8,128)S(1)}, f32[2000,256]{1,0:T(8,128)}, u32[]{:S(2)}, u32[]{:S(2)}) collective-permute-start(f32[2000,256]{1,0:T(8,128)S(1)} %copy-done.1), channel_id=1, source_target_pairs={{0,1},{1,0},{2,3},{3,2},{4,5},{5,4},{6,7},{7,6},{8,9},{9,8},{10,11... | collective-permute-start | bytes 6144008 | tf_op jit(solution)/shard_map/ppermute | solution.py:16
  (11 other events, 176.7 us)

commit v2 on v1

v2 whole, which is shorter than its diff:
```python
import jax
import jax.numpy as jnp
from jax import lax
from jax.experimental import pallas as pl
from jax.experimental.pallas import tpu as pltpu
from jax.sharding import PartitionSpec as P

D = 8192


epsilon = 1e-05
ANYWHERE = pl.BlockSpec(memory_space=pl.ANY)
SCALAR = pl.BlockSpec(memory_space=pltpu.SMEM)
ROOM = pltpu.CompilerParams(vmem_limit_bytes=56 * 2**20)


def flip(a, axis, mask):
    size = lax.axis_size(axis)
    return lax.ppermute(a, axis, [(i, i ^ mask) for i in range(size)])


def after(a, *others):
    return lax.optimization_barrier((a, *others))[0]


def normalise(hidden, norm_gain):
    values = hidden.astype(jnp.float32)
    sums = jnp.sum(values * values, axis=1)
    squares = sums + flip(sums, "narrow", 1)
    scales = lax.rsqrt(squares / D + epsilon)
    return (values * scales[:, None] * norm_gain[None, :]).astype(jnp.bfloat16)


def vocabulary_slices(row_block, parts):
    def kernel(rows_ref, slices_ref):
        width = slices_ref.shape[2]
        for part in range(parts):
            slices_ref[part] = rows_ref[:, part * width : (part + 1) * width]

    slots, vocabulary = row_block.shape
    return pl.pallas_call(
        kernel,
        out_shape=jax.ShapeDtypeStruct((parts, slots, vocabulary // parts), row_block.dtype),
        cost_estimate=pl.CostEstimate(flops=0, bytes_accessed=4 * slots * vocabulary, transcendentals=0),
        name="vocabulary_slices",
    )(row_block)


def tile_of(length):
    return max(t for t in range(16, 513, 16) if length % t == 0)


def every(count, step):
    def loop(i, _):
        step(i)
        return 0

    lax.fori_loop(0, count, loop, 0)


def rows_at(i, tile):
    return pl.ds(pl.multiple_of(i * tile, 8), tile)


def multiply(blocks, weight_t, first, begin, end):
    width = weight_t.shape[1]
    count, rows = len(blocks), blocks[0].shape[0]
    tile = tile_of(weight_t.shape[0])
    chunks = end - begin
    contract_last = (((1,), (1,)), ((), ()))

    def kernel(first_ref, *refs):
        block_refs, refs = refs[:count], refs[count:]
        weight_hbm, out_hbm, states, weight, out, state_sems, weight_sems, out_sems = refs

        def weight_copy(chunk):
            source = weight_hbm.at[rows_at(begin + chunk, tile)]
            return pltpu.make_async_copy(source, weight.at[rows_at(chunk, tile)], weight_sems.at[chunk])

        def out_copy(chunk):
            place = rows_at(chunk, tile)
            return pltpu.make_async_copy(out.at[place], out_hbm.at[place], out_sems.at[chunk])

        def one_chunk(chunk):
            weight_copy(chunk).wait()
            place = rows_at(chunk, tile)
            out[place, :] = lax.dot_general(
                weight[place, :], states[...], contract_last, preferred_element_type=jnp.float32
            )
            out_copy(chunk).start()

        state_copies = [
            pltpu.make_async_copy(
                block_refs[k],
                states.at[pl.ds(pl.multiple_of((first_ref[0] ^ k) * rows, rows), rows)],
                state_sems.at[k],
            )
            for k in range(count)
        ]
        for copy in state_copies:
            copy.start()
        every(chunks, lambda chunk: weight_copy(chunk).start())
        for copy in state_copies:
            copy.wait()
        every(chunks, one_chunk)
        every(chunks, lambda chunk: out_copy(chunk).wait())

    return pl.pallas_call(
        kernel,
        in_specs=[SCALAR] + [ANYWHERE] * (count + 1),
        out_specs=ANYWHERE,
        out_shape=jax.ShapeDtypeStruct((chunks * tile, count * rows), jnp.float32),
        scratch_shapes=[
            pltpu.VMEM((count * rows, width), jnp.bfloat16),
            pltpu.VMEM((chunks * tile, width), jnp.bfloat16),
            pltpu.VMEM((chunks * tile, count * rows), jnp.float32),
            pltpu.SemaphoreType.DMA((count,)),
            pltpu.SemaphoreType.DMA((chunks,)),
            pltpu.SemaphoreType.DMA((chunks,)),
        ],
        compiler_params=ROOM,
        cost_estimate=pl.CostEstimate(
            flops=8 * chunks * tile * width * count * rows, bytes_accessed=8 * chunks * tile * width, transcendentals=0
        ),
        name="multiply",
    )(first.reshape(1), *blocks, weight_t)


def statistics(near, near_other, far, far_other, diffs, mixing, late, parts):
    vocabulary, rows = far.shape
    slots = diffs[0].shape[1]
    tile = tile_of(vocabulary)
    chunks = vocabulary // tile
    pieces = len(near)
    contract_last = (((1,), (1,)), ((), ()))

    def kernel(late_ref, *refs):
        near_refs, near_other_refs, refs = refs[:pieces], refs[pieces : 2 * pieces], refs[2 * pieces :]
        far_ref, far_other_ref, *refs = refs
        diff_refs, mixing_refs, refs = refs[:2], refs[2:4], refs[4:]
        total_hbm, stats_ref, left, right, rows_in, mixed, left_sems, right_sems, out_sems, side_sems = refs

        def fetch(chunk, source, left_side, right_side):
            origin, place = rows_at(source, tile), rows_at(chunk, tile)
            return [
                pltpu.make_async_copy(left_side.at[origin], left.at[place], left_sems.at[chunk]),
                pltpu.make_async_copy(right_side.at[origin], right.at[place], right_sems.at[chunk]),
            ]

        def out_copy(chunk):
            place = rows_at(chunk, tile)
            return pltpu.make_async_copy(left.at[place], total_hbm.at[place], out_sems.at[chunk])

        def start_all(first, left_side, right_side):
            def start(chunk):
                for copy in fetch(first + chunk, chunk, left_side, right_side):
                    copy.start()

            every(left_side.shape[0] // tile, start)

        side_copies = [
            pltpu.make_async_copy(source, into.at[n], side_sems.at[side, n])
            for side, (sources, into) in enumerate(((mixing_refs, mixed), (diff_refs, rows_in)))
            for n, source in enumerate(sources)
        ]
        for copy in side_copies:
            copy.start()

        @pl.when(late_ref[0] == 0)
        def _():
            first = 0
            for left_side, right_side in zip(near_refs, near_other_refs):
                start_all(first, left_side, right_side)
                first += left_side.shape[0] // tile

        @pl.when(late_ref[0] == 1)
        def _():
            start_all(0, far_ref, far_other_ref)

        for copy in side_copies:
            copy.wait()

        def step(chunk, state):
            for copy in fetch(chunk, chunk, far_ref, far_other_ref):
                copy.wait()
            place = rows_at(chunk, tile)
            total = left[place, :] + right[place, :]
            for n in range(2):
                total += lax.dot_general(
                    rows_in[n, place, :], mixed[n], contract_last, preferred_element_type=jnp.float32
                )
            left[place, :] = total
            out_copy(chunk).start()
            before, mass = state
            peak = jnp.maximum(before, jnp.max(total, axis=0, keepdims=True))
            total = left[place, :]
            mass = mass * jnp.exp(before - peak) + jnp.sum(jnp.exp(total - peak), axis=0, keepdims=True)
            return peak, mass

        state = (jnp.full((1, rows), -jnp.inf, jnp.float32), jnp.zeros((1, rows), jnp.float32))
        both = jnp.concatenate(lax.fori_loop(0, chunks, step, state))
        stats_ref[...] = jnp.broadcast_to(both[None], stats_ref.shape)
        every(chunks, lambda chunk: out_copy(chunk).wait())

    return pl.pallas_call(
        kernel,
        in_specs=[SCALAR] + [ANYWHERE] * (2 * pieces + 6),
        out_specs=[ANYWHERE, pl.BlockSpec(memory_space=pltpu.VMEM)],
        out_shape=[
            jax.ShapeDtypeStruct((vocabulary, rows), jnp.float32),
            jax.ShapeDtypeStruct((parts, 2, rows), jnp.float32),
        ],
        scratch_shapes=[pltpu.VMEM((vocabulary, rows), jnp.float32)] * 2
        + [pltpu.VMEM((2, vocabulary, slots), jnp.bfloat16), pltpu.VMEM((2, rows, slots), jnp.bfloat16)]
        + [pltpu.SemaphoreType.DMA((chunks,))] * 3
        + [pltpu.SemaphoreType.DMA((2, 2))],
        compiler_params=ROOM,
        cost_estimate=pl.CostEstimate(
            flops=4 * vocabulary * rows, bytes_accessed=16 * vocabulary * rows, transcendentals=vocabulary * rows
        ),
        name="statistics",
    )(late.reshape(1), *near, *near_other, far, far_other, *diffs, *mixing)


def subtract(total, arrived):
    vocabulary, rows = total.shape
    tile = tile_of(vocabulary)
    chunks = vocabulary // tile

    def kernel(total_hbm, arrived_hbm, out_hbm, held, arrived_ref, in_sems, out_sems, arrived_sem):
        def in_copy(chunk):
            place = rows_at(chunk, tile)
            return pltpu.make_async_copy(total_hbm.at[place], held.at[place], in_sems.at[chunk])

        def out_copy(chunk):
            place = rows_at(chunk, tile)
            return pltpu.make_async_copy(held.at[place], out_hbm.at[place], out_sems.at[chunk])

        arrived_copy = pltpu.make_async_copy(arrived_hbm, arrived_ref, arrived_sem)
        arrived_copy.start()
        every(chunks, lambda chunk: in_copy(chunk).start())
        arrived_copy.wait()
        peaks, masses = arrived_ref[:, 0, :], arrived_ref[:, 1, :]
        row_peak = jnp.max(peaks, axis=0, keepdims=True)
        row_mass = jnp.sum(masses * jnp.exp(peaks - row_peak), axis=0, keepdims=True)
        log_total = row_peak + jnp.log(row_mass)

        def shift(chunk):
            in_copy(chunk).wait()
            place = rows_at(chunk, tile)
            held[place, :] = held[place, :] - log_total
            out_copy(chunk).start()

        every(chunks, shift)
        every(chunks, lambda chunk: out_copy(chunk).wait())

    return pl.pallas_call(
        kernel,
        in_specs=[ANYWHERE] * 2,
        out_specs=ANYWHERE,
        out_shape=jax.ShapeDtypeStruct((vocabulary, rows), jnp.float32),
        scratch_shapes=[pltpu.VMEM((vocabulary, rows), jnp.float32), pltpu.VMEM(arrived.shape, jnp.float32)]
        + [pltpu.SemaphoreType.DMA((chunks,))] * 2
        + [pltpu.SemaphoreType.DMA],
        compiler_params=ROOM,
        cost_estimate=pl.CostEstimate(flops=vocabulary * rows, bytes_accessed=8 * vocabulary * rows, transcendentals=0),
        name="subtract",
    )(total, arrived)


def slot_factors(slot_code, slot_count):
    slots = slot_code.shape[2]
    active = jnp.arange(slots, dtype=jnp.int32)[None, None, :] < slot_count[:, :, None]
    return jnp.where(active, slot_code, 0).astype(jnp.float32) * 0.25


def body(hidden, norm_gain, head_weight, diff_rows, slot_request, slot_code, slot_count):
    me, core = lax.axis_index("wide"), lax.axis_index("narrow")
    parts, rows = lax.axis_size("wide"), hidden.shape[0]
    weight_t = head_weight.T

    def move(a, mask):
        return flip(a, "wide", mask)

    own = normalise(hidden, norm_gain)
    x0, y0, z1, z2 = move(own, 1), move(own, 2), move(own, 4), move(own, 8)
    slices = vocabulary_slices(after(diff_rows, own)[0, 0], parts)

    own, x0, y0, z1, slices = lax.optimization_barrier((own, x0, y0, z1, slices))
    x1, y1 = move(z1, 1), move(z1, 2)
    chosen = core * 8 * rows + jnp.arange(8 * rows, dtype=jnp.int32)
    factors = slot_factors(slot_code, slot_count)

    def mixing(which):
        targets = lax.dynamic_index_in_dim(slot_request, which, 1, False).reshape(-1)
        weights = lax.dynamic_index_in_dim(factors, which, 1, False).reshape(-1)
        return jnp.where(chosen[:, None] == targets, weights, 0.0).astype(jnp.bfloat16)

    mixings = [mixing(core), mixing(1 - core)]

    x1, y1, z2, y0, mixings = lax.optimization_barrier((x1, y1, z2, y0, mixings))
    d0, d1, z3 = move(y0, 1), move(x1, 2), move(z2, 4)

    d0, d1, z3, z2 = lax.optimization_barrier((d0, d1, z3, z2))
    x2, y2, x3, y3 = move(z2, 1), move(z2, 2), move(z3, 1), move(z3, 2)
    first, half = me & 7, me // 8
    late = half ^ core
    chunks = weight_t.shape[0] // tile_of(weight_t.shape[0])
    near = multiply([own, x0, y0, d0, z1, x1, y1, d1], weight_t, first, 0, chunks)

    x3, y3, y2, x2, near, slices = lax.optimization_barrier((x3, y3, y2, x2, near, slices))
    d2, d3 = move(y2, 1), move(x3, 2)
    near_other = flip(near, "narrow", 1)
    diffs = lax.all_to_all(slices, "wide", split_axis=0, concat_axis=0, tiled=True)

    d2, d3, near_other = lax.optimization_barrier((d2, d3, near_other))
    far = multiply([z2, x2, y2, d2, z3, x3, y3, d3], weight_t, first, 0, chunks)
    far, diffs = lax.optimization_barrier((far, diffs))
    far_other = flip(far, "narrow", 1)
    diffs = diffs.reshape(-1, weight_t.shape[0]).T
    diffs_other = flip(diffs, "narrow", 1)
    total, stats = statistics([near], [near_other], far, far_other, [diffs, diffs_other], mixings, late, parts)
    arrived = lax.all_to_all(stats, "wide", split_axis=0, concat_axis=0, tiled=True)
    return subtract(total, arrived).T


def combined_all(part, axis, combine):
    gathered = jax.tree.map(lambda a: lax.all_gather(a, axis), part)

    def take(source):
        return jax.tree.map(lambda a: lax.dynamic_index_in_dim(a, source, 0, False), gathered)

    return lax.fori_loop(
        1, lax.axis_size(axis), lambda source, state: combine(state, take(source)), take(0)
    )


def merge_pair(earlier, later):
    row_peak = jnp.maximum(earlier[0], later[0])
    summed = earlier[1] * jnp.exp(earlier[0] - row_peak) + later[1] * jnp.exp(later[0] - row_peak)
    return (row_peak, summed)


def general_body(hidden, norm_gain, head_weight, diff_rows, slot_request, slot_code, slot_count):
    values = hidden.astype(jnp.float32)
    squares = lax.psum(jnp.sum(values * values, axis=1), "narrow")
    scales = lax.rsqrt(squares / D + epsilon)
    normed = (values * scales[:, None] * norm_gain[None, :]).astype(jnp.bfloat16)
    partial_value = jnp.dot(
        lax.all_gather(normed, "wide", axis=0, tiled=True),
        head_weight,
        preferred_element_type=jnp.float32,
    )
    arrived = lax.all_to_all(diff_rows[0, 0], "wide", split_axis=1, concat_axis=0, tiled=True)
    base_block = lax.psum_scatter(partial_value, "narrow", scatter_dimension=0, tiled=True)
    owner_slices = lax.all_gather(arrived, "narrow", axis=0, tiled=True)
    targets = jnp.transpose(slot_request, (1, 0, 2)).reshape(-1)
    factor_all = jnp.transpose(slot_factors(slot_code, slot_count), (1, 0, 2)).reshape(-1)
    block_rows = base_block.shape[0]
    offsets = targets - lax.axis_index("narrow") * block_rows
    owned = (offsets >= 0) & (offsets < block_rows)
    factors = jnp.where(owned, factor_all, 0.0)
    target_rows = jnp.where(owned, offsets, 0)
    own_block = base_block.at[target_rows].add(owner_slices.astype(jnp.float32) * factors[:, None])
    local_peak = jnp.max(own_block, axis=1)
    local_mass = jnp.sum(jnp.exp(own_block - local_peak[:, None]), axis=1)
    row_peak, row_mass = combined_all((local_peak, local_mass), "wide", merge_pair)
    log_total = row_peak + jnp.log(row_mass)
    return own_block - log_total[:, None]


def solution(mesh):
    placed = (
        P("wide", "narrow"),
        P("narrow"),
        P("narrow", "wide"),
        P("wide", "narrow", None, None),
        P(),
        P(),
        P(),
    )
    small = mesh.shape["wide"] == 16 and mesh.shape["narrow"] == 2
    return jax.shard_map(
        body if small else general_body,
        mesh=mesh,
        in_specs=placed,
        out_specs=P("narrow", "wide"),
        check_vma=False,
    )
```

time: 110 us -> 94.8 us (0.86)
  waiting for transfers between devices: 34.8 us -> 20.4 us
  Pallas kernels: 30.8 us -> 27.4 us
  local copies, waits for them, and re-layouts: 2.14 us -> 4.1 us
  blocking collectives: 12.8 us -> 11.5 us
  starting transfers between devices: 25.7 us -> 27 us
    ppermute x18 -> x19, waiting for transfers between devices: 34.8 us -> 17.3 us  [flip(): return lax.ppermute(a, axis, [(i, i ^ mask) for i in range(size)])]
    pallas_call x5 -> x4, Pallas kernels: 28.8 us -> 25.4 us  [the longest x2 18.2 us: multiply(): pl.pallas_call(kernel, in_specs=[SCALAR] + [ANYWHERE] * (count + 1), out_...]
    all_to_all x1, waiting for transfers between devices: 0.01 us -> 3.09 us  [body(): lax.all_to_all(slices, 'wide', split_axis=0, concat_axis=0, tiled=True)]
    unnamed x32 -> x34, local copies, waits for them, and re-layouts: 0.76 us -> 2.41 us
    all_to_all x1, blocking collectives: 12.8 us -> 11.5 us  [body(): lax.all_to_all(stats, 'wide', split_axis=0, concat_axis=0, tiled=True)]
    all_to_all x1, starting transfers between devices: 3.97 us -> 5.14 us  [body(): lax.all_to_all(slices, 'wide', split_axis=0, concat_axis=0, tiled=True)]
    ppermute x18 -> x19, starting transfers between devices: 21.7 us -> 21.9 us  [flip(): return lax.ppermute(a, axis, [(i, i ^ mask) for i in range(size)])]
  transfers between devices with their start and end apart: 19 -> 20, of which waited for: 9 -> 10; matrix products, arithmetic and copies ran while one was open for 2% -> 3% of each run, Pallas kernels for 13% -> 21%
where the time goes in v2:
time: 94.8 us; the launch traced here: 94.4 us
  Pallas kernels  27.4 us (29%)
  starting transfers between devices  27 us (28%)
  waiting for transfers between devices  20.4 us (22%)
  blocking collectives  11.5 us (12%)
  local copies, waits for them, and re-layouts  4.1 us (4%)
  other arithmetic  3.66 us (4%)
    ppermute x19, starting transfers between devices, flip(): return lax.ppermute(a, axis, [(i, i ^ mask) for i in range(size)])  21.9 us
    pallas_call x2, Pallas kernels, multiply(): pl.pallas_call(kernel, in_specs=[SCALAR] + [ANYWHERE] * (count + 1), out_...  18.2 us
    ppermute x19, waiting for transfers between devices, flip(): return lax.ppermute(a, axis, [(i, i ^ mask) for i in range(size)])  17.3 us
    all_to_all x1, blocking collectives, body(): lax.all_to_all(stats, 'wide', split_axis=0, concat_axis=0, tiled=True)  11.5 us
    all_to_all x1, starting transfers between devices, body(): lax.all_to_all(slices, 'wide', split_axis=0, concat_axis=0, tiled=True)  5.14 us
    pallas_call x1, Pallas kernels, statistics(): pl.pallas_call(kernel, in_specs=[SCALAR] + [ANYWHERE] * (2 * pieces + 6),...  4.77 us
    all_to_all x1, waiting for transfers between devices, body(): lax.all_to_all(slices, 'wide', split_axis=0, concat_axis=0, tiled=True)  3.09 us
    pallas_call x1, Pallas kernels, subtract(): pl.pallas_call(kernel, in_specs=[ANYWHERE] * 2, out_specs=ANYWHERE, out_s...  2.43 us
  transfers between devices with their start and end apart: 20, of which 10 were waited for; matrix products, arithmetic and copies ran while one was open for 3% of the time, Pallas kernels for 21%

profile of v2, /device:TPU:0, one launch (start us, length us, event | category | flops | bytes accessed | tf_op | source)
XLA Modules:
  0.0 94.4 jit_solution(1888477277282080268)
XLA Ops:
  0.0 1.1 %fusion = f32[32]{0:T(128)S(1)} fusion(bf16[32,4096]{1,0:T(8,128)(2,1)} %param.7), kind=kLoop, calls=%fused_computation.2 | loop fusion | flops 393184 | bytes 262272 | tf_op jit(solution)/shard_map/reduce_sum | solution.py:28
  3.5 2.9 %collective-permute-start.3 = (bf16[32,4096]{1,0:T(8,128)(2,1)S(1)}, bf16[32,4096]{1,0:T(8,128)(2,1)S(1)}, u32[]{:S(2)}, u32[]{:S(2)}) collective-permute-start(bf16[32,4096]{1,0:T(8,128)(2,1)S(1)} %fusion.2.refs_0_), channel_id=1, source_target_pairs={{0,8},{2,10},{4,12},{6,14},{8,0},{10,2},{12,4},{14,6},{16,24},{18,... | collective-permute-start | bytes 786440 | tf_op jit(solution)/shard_map/ppermute | solution.py:19
  6.5 1.5 %collective-permute-start.2 = (bf16[32,4096]{1,0:T(8,128)(2,1)S(1)}, bf16[32,4096]{1,0:T(8,128)(2,1)S(1)}, u32[]{:S(2)}, u32[]{:S(2)}) collective-permute-start(bf16[32,4096]{1,0:T(8,128)(2,1)S(1)} %fusion.2.refs_0_), channel_id=1, source_target_pairs={{0,4},{2,6},{4,0},{6,2},{8,12},{10,14},{12,8},{14,10},{16,20},{18,... | collective-permute-start | bytes 786440 | tf_op jit(solution)/shard_map/ppermute | solution.py:19
  8.0 1.5 %collective-permute-start.1 = (bf16[32,4096]{1,0:T(8,128)(2,1)S(1)}, bf16[32,4096]{1,0:T(8,128)(2,1)S(1)}, u32[]{:S(2)}, u32[]{:S(2)}) collective-permute-start(bf16[32,4096]{1,0:T(8,128)(2,1)S(1)} %fusion.2.refs_0_), channel_id=1, source_target_pairs={{0,2},{2,0},{4,6},{6,4},{8,10},{10,8},{12,14},{14,12},{16,18},{18,... | collective-permute-start | bytes 786440 | tf_op jit(solution)/shard_map/ppermute | solution.py:19
  10.9 2.6 %collective-permute-start.6 = (bf16[32,4096]{1,0:T(8,128)(2,1)S(1)}, bf16[32,4096]{1,0:T(8,128)(2,1)S(1)}, u32[]{:S(2)}, u32[]{:S(2)}) collective-permute-start(bf16[32,4096]{1,0:T(8,128)(2,1)S(1)} %fusion.2.refs_0_), channel_id=1, source_target_pairs={{0,16},{2,18},{4,20},{6,22},{8,24},{10,26},{12,28},{14,30},{16,0},... | collective-permute-start | bytes 786440 | tf_op jit(solution)/shard_map/ppermute | solution.py:19
  13.5 2.0 %vocabulary_slices.1 = bf16[16,8,2000]{2,1,0:T(8,128)(2,1)} custom-call(bf16[8,32000]{1,0:T(8,128)(2,1)} %bitcast.18), custom_call_target="tpu_custom_call" | custom-call | bytes 1024000 | tf_op jit(solution)/shard_map/vocabulary_slices/pallas_call | solution.py:41
  15.9 1.4 %collective-permute-start.5 = (bf16[32,4096]{1,0:T(8,128)(2,1)S(1)}, bf16[32,4096]{1,0:T(8,128)(2,1)S(1)}, u32[]{:S(2)}, u32[]{:S(2)}) collective-permute-start(bf16[32,4096]{1,0:T(8,128)(2,1)S(1)} %collective-permute-done.3.refs_4_), channel_id=1, source_target_pairs={{0,4},{2,6},{4,0},{6,2},{8,12},{10,14},{12,8},{14,10},{16,20},{18,... | collective-permute-start | bytes 786440 | tf_op jit(solution)/shard_map/ppermute | solution.py:19
  17.3 2.8 %collective-permute-start.4 = (bf16[32,4096]{1,0:T(8,128)(2,1)S(1)}, bf16[32,4096]{1,0:T(8,128)(2,1)S(1)}, u32[]{:S(2)}, u32[]{:S(2)}) collective-permute-start(bf16[32,4096]{1,0:T(8,128)(2,1)S(1)} %collective-permute-done.3.refs_4_), channel_id=1, source_target_pairs={{0,2},{2,0},{4,6},{6,4},{8,10},{10,8},{12,14},{14,12},{16,18},{18,... | collective-permute-start | bytes 786440 | tf_op jit(solution)/shard_map/ppermute | solution.py:19
  21.5 3.5 %collective-permute-done.6.refs_0_ = bf16[32,4096]{1,0:T(8,128)(2,1)S(1)} collective-permute-done((bf16[32,4096]{1,0:T(8,128)(2,1)S(1)}, bf16[32,4096]{1,0:T(8,128)(2,1)S(1)}, u32[]{:S(2)}, u32[]{:S(2)}) %collective-permute-start.6) | collective-permute-done | bytes 262176 | tf_op jit(solution)/shard_map/ppermute | solution.py:19
  25.5 1.7 %collective-permute-start.7 = (bf16[32,4096]{1,0:T(8,128)(2,1)S(1)}, bf16[32,4096]{1,0:T(8,128)(2,1)S(1)}, u32[]{:S(2)}, u32[]{:S(2)}) collective-permute-start(bf16[32,4096]{1,0:T(8,128)(2,1)S(1)} %collective-permute-done.2.refs_2_), channel_id=1, source_target_pairs={{0,2},{2,0},{4,6},{6,4},{8,10},{10,8},{12,14},{14,12},{16,18},{18,... | collective-permute-start | bytes 786440 | tf_op jit(solution)/shard_map/ppermute | solution.py:19
  27.6 4.5 %collective-permute-done.7.refs_3_ = bf16[32,4096]{1,0:T(8,128)(2,1)S(1)} collective-permute-done((bf16[32,4096]{1,0:T(8,128)(2,1)S(1)}, bf16[32,4096]{1,0:T(8,128)(2,1)S(1)}, u32[]{:S(2)}, u32[]{:S(2)}) %collective-permute-start.7) | collective-permute-done | bytes 262176 | tf_op jit(solution)/shard_map/ppermute | solution.py:19
  32.1 1.5 %collective-permute-done.8.refs_7_ = bf16[32,4096]{1,0:T(8,128)(2,1)S(1)} collective-permute-done((bf16[32,4096]{1,0:T(8,128)(2,1)S(1)}, bf16[32,4096]{1,0:T(8,128)(2,1)S(1)}, u32[]{:S(2)}, u32[]{:S(2)}) %collective-permute-start.8) | collective-permute-done | bytes 262176 | tf_op jit(solution)/shard_map/ppermute | solution.py:19
  34.0 1.7 %collective-permute-start.11 = (bf16[32,4096]{1,0:T(8,128)(2,1)S(1)}, bf16[32,4096]{1,0:T(8,128)(2,1)S(1)}, u32[]{:S(2)}, u32[]{:S(2)}) collective-permute-start(bf16[32,4096]{1,0:T(8,128)(2,1)S(1)} %collective-permute-done.9.refs_4_), channel_id=1, source_target_pairs={{0,4},{2,6},{4,0},{6,2},{8,12},{10,14},{12,8},{14,10},{16,20},{18,... | collective-permute-start | bytes 786440 | tf_op jit(solution)/shard_map/ppermute | solution.py:19
  35.9 1.7 %collective-permute-start.13 = (bf16[32,4096]{1,0:T(8,128)(2,1)S(1)}, bf16[32,4096]{1,0:T(8,128)(2,1)S(1)}, u32[]{:S(2)}, u32[]{:S(2)}) collective-permute-start(bf16[32,4096]{1,0:T(8,128)(2,1)S(1)} %collective-permute-done.6.refs_0_), channel_id=1, source_target_pairs={{0,2},{2,0},{4,6},{6,4},{8,10},{10,8},{12,14},{14,12},{16,18},{18,... | collective-permute-start | bytes 786440 | tf_op jit(solution)/shard_map/ppermute | solution.py:19
  38.1 8.7 %multiply.5.refs_0_ = f32[2000,256]{1,0:T(8,128)} custom-call(s32[1]{0:T(128)} %bitcast.2.first_ref, bf16[32,4096]{1,0:T(8,128)(2,1)} %copy-done.3, bf16[32,4096]{1,0:T(8,128)(2,1)} %copy-done.7, bf16[32,4096]{1,0:T(8,128)(2,1)} %copy-done.6, bf16[32,4096]{1,0:T(8,128)(2,1)} %copy-done.13, bf16[32,4096]{1,0:T(8,128)(2,1)} %copy-done.5, ...), custom_call_target="tpu_custom_call" | custom-call | flops 16777216000 | bytes 65536000 | tf_op jit(solution)/shard_map/multiply/pallas_call | solution.py:108
  48.0 1.7 %collective-permute-start.15 = (bf16[32,4096]{1,0:T(8,128)(2,1)}, bf16[32,4096]{1,0:T(8,128)(2,1)S(1)}, u32[]{:S(2)}, u32[]{:S(2)}) collective-permute-start(bf16[32,4096]{1,0:T(8,128)(2,1)} %collective-permute-done.10.refs_5_), channel_id=1, source_target_pairs={{0,4},{2,6},{4,0},{6,2},{8,12},{10,14},{12,8},{14,10},{16,20},{18,... | collective-permute-start | bytes 786440 | tf_op jit(solution)/shard_map/ppermute | solution.py:19
  49.6 5.1 %all-to-all-start = ((bf16[16,8,2000]{2,1,0:T(8,128)(2,1)}), bf16[16,8,2000]{2,1,0:T(8,128)(2,1)S(1)}, u32[]{:S(2)}, u32[]{:S(2)}) async-start(bf16[16,8,2000]{2,1,0:T(8,128)(2,1)} %vocabulary_slices.1), calls=%async_computation | async-start | bytes 1048576 | tf_op jit(solution)/shard_map/all_to_all | solution.py:314
  54.8 1.8 %collective-permute-done.14.refs_3_ = bf16[32,4096]{1,0:T(8,128)(2,1)S(1)} collective-permute-done((bf16[32,4096]{1,0:T(8,128)(2,1)}, bf16[32,4096]{1,0:T(8,128)(2,1)S(1)}, u32[]{:S(2)}, u32[]{:S(2)}) %collective-permute-start.14) | collective-permute-done | bytes 262176 | tf_op jit(solution)/shard_map/ppermute | solution.py:19
  57.4 9.4 %multiply.6.refs_2_ = f32[2000,256]{1,0:T(8,128)} custom-call(s32[1]{0:T(128)} %bitcast.2.first_ref, bf16[32,4096]{1,0:T(8,128)(2,1)} %copy-done.4, bf16[32,4096]{1,0:T(8,128)(2,1)} %copy-done.12, bf16[32,4096]{1,0:T(8,128)(2,1)} %collective-permute-done.12.refs_2_, bf16[32,4096]{1,0:T(8,128)(2,1)} %copy-done.15, bf16[32,4096]{1,0:T(8,128)(2,1)} %copy-done.10, ...), custom_call_target="tpu_custom_call" | custom-call | flops 16777216000 | bytes 65536000 | tf_op jit(solution)/shard_map/multiply/pallas_call | solution.py:108
  66.9 3.1 %all-to-all-done = bf16[16,8,2000]{2,1,0:T(8,128)(2,1)S(1)} async-done(((bf16[16,8,2000]{2,1,0:T(8,128)(2,1)}), bf16[16,8,2000]{2,1,0:T(8,128)(2,1)S(1)}, u32[]{:S(2)}, u32[]{:S(2)}) %all-to-all-start) | async-done | bytes 512032 | tf_op jit(solution)/shard_map/all_to_all | solution.py:314
  70.9 3.9 %collective-permute-done.18.refs_5_ = bf16[2000,128]{1,0:T(8,128)(2,1)S(1)} collective-permute-done((bf16[2000,128]{1,0:T(8,128)(2,1)S(1)}, bf16[2000,128]{1,0:T(8,128)(2,1)S(1)}, u32[]{:S(2)}, u32[]{:S(2)}) %collective-permute-start.18) | collective-permute-done | bytes 512032 | tf_op jit(solution)/shard_map/ppermute | solution.py:19
  75.6 4.8 %statistics.1 = (f32[2000,256]{1,0:T(8,128)}, f32[16,2,256]{2,1,0:T(2,128)}) custom-call(s32[1]{0:T(128)} %bitcast.late_ref, f32[2000,256]{1,0:T(8,128)} %multiply.5.refs_0_, f32[2000,256]{1,0:T(8,128)} %copy-done.1, f32[2000,256]{1,0:T(8,128)} %multiply.6.refs_2_, f32[2000,256]{1,0:T(8,128)} %collective-permute-done.17.refs_3_, bf16[2000,128]{1,0:T(8,128)(2,1)} %bitcast.17, ...), custom_call_target="tpu_custom_call" | custom-call | flops 2048000 | bytes 8192000 | tf_op jit(solution)/shard_map/statistics/pallas_call | solution.py:205
  80.4 11.5 %all_to_all.10.arrived_hbm = f32[16,2,256]{2,1,0:T(2,128)} all-to-all(f32[16,2,256]{2,1,0:T(2,128)} %get-tuple-element.62), channel_id=1, replica_groups=mesh['wide'=16,'narrow'=2] {'wide'}, dimensions={0} | all-to-all | bytes 65536 | tf_op jit(solution)/shard_map/all_to_all | solution.py:323
  91.9 2.4 %subtract.2 = f32[2000,256]{1,0:T(8,128)} custom-call(f32[2000,256]{1,0:T(8,128)} %get-tuple-element.61.total_hbm, f32[16,2,256]{2,1,0:T(2,128)} %all_to_all.10.arrived_hbm), custom_call_target="tpu_custom_call" | custom-call | flops 512000 | bytes 4096000 | tf_op jit(solution)/shard_map/subtract/pallas_call | solution.py:257
  (73 shorter events, 11.0 us)
Async XLA Ops:
  1.1 1.3 %collective-permute-start = (f32[32]{0:T(128)S(1)}, f32[32]{0:T(128)S(1)}, u32[]{:S(2)}, u32[]{:S(2)}) collective-permute-start(f32[32]{0:T(128)S(1)} %fusion), channel_id=1, source_target_pairs={{0,1},{1,0},{2,3},{3,2},{4,5},{5,4},{6,7},{7,6},{8,9},{9,8},{10,11... | collective-permute-start | bytes 392 | tf_op jit(solution)/shard_map/ppermute | solution.py:19
  3.5 34.5 %copy-start.3 = (bf16[32,4096]{1,0:T(8,128)(2,1)}, bf16[32,4096]{1,0:T(8,128)(2,1)S(1)}, u32[]{:S(2)}) copy-start(bf16[32,4096]{1,0:T(8,128)(2,1)S(1)} %fusion.2.refs_0_) | copy-start | bytes 786436
  3.5 12.0 %collective-permute-start.3 = (bf16[32,4096]{1,0:T(8,128)(2,1)S(1)}, bf16[32,4096]{1,0:T(8,128)(2,1)S(1)}, u32[]{:S(2)}, u32[]{:S(2)}) collective-permute-start(bf16[32,4096]{1,0:T(8,128)(2,1)S(1)} %fusion.2.refs_0_), channel_id=1, source_target_pairs={{0,8},{2,10},{4,12},{6,14},{8,0},{10,2},{12,4},{14,6},{16,24},{18,... | collective-permute-start | bytes 786440 | tf_op jit(solution)/shard_map/ppermute | solution.py:19
  6.5 9.1 %collective-permute-start.2 = (bf16[32,4096]{1,0:T(8,128)(2,1)S(1)}, bf16[32,4096]{1,0:T(8,128)(2,1)S(1)}, u32[]{:S(2)}, u32[]{:S(2)}) collective-permute-start(bf16[32,4096]{1,0:T(8,128)(2,1)S(1)} %fusion.2.refs_0_), channel_id=1, source_target_pairs={{0,4},{2,6},{4,0},{6,2},{8,12},{10,14},{12,8},{14,10},{16,20},{18,... | collective-permute-start | bytes 786440 | tf_op jit(solution)/shard_map/ppermute | solution.py:19
  8.0 7.9 %collective-permute-start.1 = (bf16[32,4096]{1,0:T(8,128)(2,1)S(1)}, bf16[32,4096]{1,0:T(8,128)(2,1)S(1)}, u32[]{:S(2)}, u32[]{:S(2)}) collective-permute-start(bf16[32,4096]{1,0:T(8,128)(2,1)S(1)} %fusion.2.refs_0_), channel_id=1, source_target_pairs={{0,2},{2,0},{4,6},{6,4},{8,10},{10,8},{12,14},{14,12},{16,18},{18,... | collective-permute-start | bytes 786440 | tf_op jit(solution)/shard_map/ppermute | solution.py:19
  10.9 14.1 %collective-permute-start.6 = (bf16[32,4096]{1,0:T(8,128)(2,1)S(1)}, bf16[32,4096]{1,0:T(8,128)(2,1)S(1)}, u32[]{:S(2)}, u32[]{:S(2)}) collective-permute-start(bf16[32,4096]{1,0:T(8,128)(2,1)S(1)} %fusion.2.refs_0_), channel_id=1, source_target_pairs={{0,16},{2,18},{4,20},{6,22},{8,24},{10,26},{12,28},{14,30},{16,0},... | collective-permute-start | bytes 786440 | tf_op jit(solution)/shard_map/ppermute | solution.py:19
  15.5 22.5 %copy-start.5 = (bf16[32,4096]{1,0:T(8,128)(2,1)}, bf16[32,4096]{1,0:T(8,128)(2,1)S(1)}, u32[]{:S(2)}) copy-start(bf16[32,4096]{1,0:T(8,128)(2,1)S(1)} %collective-permute-done.3.refs_4_) | copy-start | bytes 786436
  15.6 22.5 %copy-start.6 = (bf16[32,4096]{1,0:T(8,128)(2,1)}, bf16[32,4096]{1,0:T(8,128)(2,1)S(1)}, u32[]{:S(2)}) copy-start(bf16[32,4096]{1,0:T(8,128)(2,1)S(1)} %collective-permute-done.2.refs_2_) | copy-start | bytes 786436
  15.9 22.2 %copy-start.7 = (bf16[32,4096]{1,0:T(8,128)(2,1)}, bf16[32,4096]{1,0:T(8,128)(2,1)S(1)}, u32[]{:S(2)}) copy-start(bf16[32,4096]{1,0:T(8,128)(2,1)S(1)} %collective-permute-done.1.refs_1_) | copy-start | bytes 786436
  15.9 9.1 %collective-permute-start.5 = (bf16[32,4096]{1,0:T(8,128)(2,1)S(1)}, bf16[32,4096]{1,0:T(8,128)(2,1)S(1)}, u32[]{:S(2)}, u32[]{:S(2)}) collective-permute-start(bf16[32,4096]{1,0:T(8,128)(2,1)S(1)} %collective-permute-done.3.refs_4_), channel_id=1, source_target_pairs={{0,4},{2,6},{4,0},{6,2},{8,12},{10,14},{12,8},{14,10},{16,20},{18,... | collective-permute-start | bytes 786440 | tf_op jit(solution)/shard_map/ppermute | solution.py:19
  17.3 8.2 %collective-permute-start.4 = (bf16[32,4096]{1,0:T(8,128)(2,1)S(1)}, bf16[32,4096]{1,0:T(8,128)(2,1)S(1)}, u32[]{:S(2)}, u32[]{:S(2)}) collective-permute-start(bf16[32,4096]{1,0:T(8,128)(2,1)S(1)} %collective-permute-done.3.refs_4_), channel_id=1, source_target_pairs={{0,2},{2,0},{4,6},{6,4},{8,10},{10,8},{12,14},{14,12},{16,18},{18,... | collective-permute-start | bytes 786440 | tf_op jit(solution)/shard_map/ppermute | solution.py:19
  25.5 6.6 %collective-permute-start.7 = (bf16[32,4096]{1,0:T(8,128)(2,1)S(1)}, bf16[32,4096]{1,0:T(8,128)(2,1)S(1)}, u32[]{:S(2)}, u32[]{:S(2)}) collective-permute-start(bf16[32,4096]{1,0:T(8,128)(2,1)S(1)} %collective-permute-done.2.refs_2_), channel_id=1, source_target_pairs={{0,2},{2,0},{4,6},{6,4},{8,10},{10,8},{12,14},{14,12},{16,18},{18,... | collective-permute-start | bytes 786440 | tf_op jit(solution)/shard_map/ppermute | solution.py:19
  27.2 6.4 %collective-permute-start.8 = (bf16[32,4096]{1,0:T(8,128)(2,1)S(1)}, bf16[32,4096]{1,0:T(8,128)(2,1)S(1)}, u32[]{:S(2)}, u32[]{:S(2)}) collective-permute-start(bf16[32,4096]{1,0:T(8,128)(2,1)S(1)} %collective-permute-done.4.refs_5_), channel_id=1, source_target_pairs={{0,4},{2,6},{4,0},{6,2},{8,12},{10,14},{12,8},{14,10},{16,20},{18,... | collective-permute-start | bytes 786440 | tf_op jit(solution)/shard_map/ppermute | solution.py:19
  27.6 6.4 %collective-permute-start.9 = (bf16[32,4096]{1,0:T(8,128)(2,1)S(1)}, bf16[32,4096]{1,0:T(8,128)(2,1)S(1)}, u32[]{:S(2)}, u32[]{:S(2)}) collective-permute-start(bf16[32,4096]{1,0:T(8,128)(2,1)S(1)} %collective-permute-done.6.refs_0_), channel_id=1, source_target_pairs={{0,8},{2,10},{4,12},{6,14},{8,0},{10,2},{12,4},{14,6},{16,24},{18,... | collective-permute-start | bytes 786440 | tf_op jit(solution)/shard_map/ppermute | solution.py:19
  34.0 12.9 %collective-permute-start.11 = (bf16[32,4096]{1,0:T(8,128)(2,1)S(1)}, bf16[32,4096]{1,0:T(8,128)(2,1)S(1)}, u32[]{:S(2)}, u32[]{:S(2)}) collective-permute-start(bf16[32,4096]{1,0:T(8,128)(2,1)S(1)} %collective-permute-done.9.refs_4_), channel_id=1, source_target_pairs={{0,4},{2,6},{4,0},{6,2},{8,12},{10,14},{12,8},{14,10},{16,20},{18,... | collective-permute-start | bytes 786440 | tf_op jit(solution)/shard_map/ppermute | solution.py:19
  35.6 11.2 %collective-permute-start.10 = (bf16[32,4096]{1,0:T(8,128)(2,1)S(1)}, bf16[32,4096]{1,0:T(8,128)(2,1)}, u32[]{:S(2)}, u32[]{:S(2)}) collective-permute-start(bf16[32,4096]{1,0:T(8,128)(2,1)S(1)} %collective-permute-done.9.refs_4_), channel_id=1, source_target_pairs={{0,2},{2,0},{4,6},{6,4},{8,10},{10,8},{12,14},{14,12},{16,18},{18,... | collective-permute-start | bytes 786440 | tf_op jit(solution)/shard_map/ppermute | solution.py:19
  35.9 10.9 %collective-permute-start.13 = (bf16[32,4096]{1,0:T(8,128)(2,1)S(1)}, bf16[32,4096]{1,0:T(8,128)(2,1)S(1)}, u32[]{:S(2)}, u32[]{:S(2)}) collective-permute-start(bf16[32,4096]{1,0:T(8,128)(2,1)S(1)} %collective-permute-done.6.refs_0_), channel_id=1, source_target_pairs={{0,2},{2,0},{4,6},{6,4},{8,10},{10,8},{12,14},{14,12},{16,18},{18,... | collective-permute-start | bytes 786440 | tf_op jit(solution)/shard_map/ppermute | solution.py:19
  37.7 10.0 %collective-permute-start.12 = (bf16[32,4096]{1,0:T(8,128)(2,1)S(1)}, bf16[32,4096]{1,0:T(8,128)(2,1)}, u32[]{:S(2)}, u32[]{:S(2)}) collective-permute-start(bf16[32,4096]{1,0:T(8,128)(2,1)S(1)} %collective-permute-done.6.refs_0_), channel_id=1, source_target_pairs={{0,4},{2,6},{4,0},{6,2},{8,12},{10,14},{12,8},{14,10},{16,20},{18,... | collective-permute-start | bytes 786440 | tf_op jit(solution)/shard_map/ppermute | solution.py:19
  47.7 8.9 %collective-permute-start.16 = (f32[2000,256]{1,0:T(8,128)}, f32[2000,256]{1,0:T(8,128)S(1)}, u32[]{:S(2)}, u32[]{:S(2)}) collective-permute-start(f32[2000,256]{1,0:T(8,128)} %multiply.5.refs_0_), channel_id=1, source_target_pairs={{0,1},{1,0},{2,3},{3,2},{4,5},{5,4},{6,7},{7,6},{8,9},{9,8},{10,11... | collective-permute-start | bytes 6144008 | tf_op jit(solution)/shard_map/ppermute | solution.py:19
  47.7 8.9 %collective-permute-start.14 = (bf16[32,4096]{1,0:T(8,128)(2,1)}, bf16[32,4096]{1,0:T(8,128)(2,1)S(1)}, u32[]{:S(2)}, u32[]{:S(2)}) collective-permute-start(bf16[32,4096]{1,0:T(8,128)(2,1)} %collective-permute-done.12.refs_2_), channel_id=1, source_target_pairs={{0,2},{2,0},{4,6},{6,4},{8,10},{10,8},{12,14},{14,12},{16,18},{18,... | collective-permute-start | bytes 786440 | tf_op jit(solution)/shard_map/ppermute | solution.py:19
  48.0 8.6 %collective-permute-start.15 = (bf16[32,4096]{1,0:T(8,128)(2,1)}, bf16[32,4096]{1,0:T(8,128)(2,1)S(1)}, u32[]{:S(2)}, u32[]{:S(2)}) collective-permute-start(bf16[32,4096]{1,0:T(8,128)(2,1)} %collective-permute-done.10.refs_5_), channel_id=1, source_target_pairs={{0,4},{2,6},{4,0},{6,2},{8,12},{10,14},{12,8},{14,10},{16,20},{18,... | collective-permute-start | bytes 786440 | tf_op jit(solution)/shard_map/ppermute | solution.py:19
  49.6 20.4 %all-to-all-start = ((bf16[16,8,2000]{2,1,0:T(8,128)(2,1)}), bf16[16,8,2000]{2,1,0:T(8,128)(2,1)S(1)}, u32[]{:S(2)}, u32[]{:S(2)}) async-start(bf16[16,8,2000]{2,1,0:T(8,128)(2,1)} %vocabulary_slices.1), calls=%async_computation | async-start | bytes 1048576 | tf_op jit(solution)/shard_map/all_to_all | solution.py:314
  70.0 4.8 %collective-permute-start.17 = (f32[2000,256]{1,0:T(8,128)}, f32[2000,256]{1,0:T(8,128)}, u32[]{:S(2)}, u32[]{:S(2)}) collective-permute-start(f32[2000,256]{1,0:T(8,128)} %multiply.6.refs_2_), channel_id=1, source_target_pairs={{0,1},{1,0},{2,3},{3,2},{4,5},{5,4},{6,7},{7,6},{8,9},{9,8},{10,11... | collective-permute-start | bytes 6144008 | tf_op jit(solution)/shard_map/ppermute | solution.py:19
  70.3 4.5 %collective-permute-start.18 = (bf16[2000,128]{1,0:T(8,128)(2,1)S(1)}, bf16[2000,128]{1,0:T(8,128)(2,1)S(1)}, u32[]{:S(2)}, u32[]{:S(2)}) collective-permute-start(bf16[2000,128]{1,0:T(8,128)(2,1)S(1)} %bitcast.16), channel_id=1, source_target_pairs={{0,1},{1,0},{2,3},{3,2},{4,5},{5,4},{6,7},{7,6},{8,9},{9,8},{10,11... | collective-permute-start | bytes 1536008 | tf_op jit(solution)/shard_map/ppermute | solution.py:19
  (13 other events, 97.5 us)

commit v3 on v2

--- a/solution.py
+++ b/solution.py
@@ -46,6 +46,10 @@
     )(row_block)
 
 
+def in_hbm(a):
+    return pltpu.with_memory_space_constraint(a, pltpu.HBM)
+
+
 def tile_of(length):
     return max(t for t in range(16, 513, 16) if length % t == 0)
 
@@ -62,24 +66,27 @@
     return pl.ds(pl.multiple_of(i * tile, 8), tile)
 
 
-def multiply(blocks, weight_t, first, begin, end):
+def multiply(blocks, weight_t, first, pieces):
     width = weight_t.shape[1]
     count, rows = len(blocks), blocks[0].shape[0]
     tile = tile_of(weight_t.shape[0])
-    chunks = end - begin
+    chunks = sum(pieces)
+    begins = [sum(pieces[:n]) for n in range(len(pieces))]
     contract_last = (((1,), (1,)), ((), ()))
 
     def kernel(first_ref, *refs):
         block_refs, refs = refs[:count], refs[count:]
-        weight_hbm, out_hbm, states, weight, out, state_sems, weight_sems, out_sems = refs
+        weight_hbm, out_hbms, refs = refs[0], refs[1 : 1 + len(pieces)], refs[1 + len(pieces) :]
+        states, weight, out, state_sems, weight_sems, out_sems = refs
 
         def weight_copy(chunk):
-            source = weight_hbm.at[rows_at(begin + chunk, tile)]
-            return pltpu.make_async_copy(source, weight.at[rows_at(chunk, tile)], weight_sems.at[chunk])
-
-        def out_copy(chunk):
-            place = rows_at(chunk, tile)
-            return pltpu.make_async_copy(out.at[place], out_hbm.at[place], out_sems.at[chunk])
+            place = rows_at(chunk, tile)
+            return pltpu.make_async_copy(weight_hbm.at[place], weight.at[place], weight_sems.at[chunk])
+
+        def out_copy(piece, chunk):
+            source = out.at[rows_at(begins[piece] + chunk, tile)]
+            target = out_hbms[piece].at[rows_at(chunk, tile)]
+            return pltpu.make_async_copy(source, target, out_sems.at[begins[piece] + chunk])
 
         def one_chunk(chunk):
             weight_copy(chunk).wait()
@@ -87,7 +94,11 @@
             out[place, :] = lax.dot_general(
                 weight[place, :], states[...], contract_last, preferred_element_type=jnp.float32
             )
-            out_copy(chunk).start()
+            for piece, (begin, length) in enumerate(zip(begins, pieces)):
+
+                @pl.when((chunk >= begin) & (chunk < begin + length))
+                def _():
+                    out_copy(piece, chunk - begin).start()
 
         state_copies = [
             pltpu.make_async_copy(
@@ -103,13 +114,14 @@
         for copy in state_copies:
             copy.wait()
         every(chunks, one_chunk)
-        every(chunks, lambda chunk: out_copy(chunk).wait())
+        for piece, length in enumerate(pieces):
+            every(length, lambda chunk, piece=piece: out_copy(piece, chunk).wait())
 
     return pl.pallas_call(
         kernel,
         in_specs=[SCALAR] + [ANYWHERE] * (count + 1),
-        out_specs=ANYWHERE,
-        out_shape=jax.ShapeDtypeStruct((chunks * tile, count * rows), jnp.float32),
+        out_specs=[ANYWHERE] * len(pieces),
+        out_shape=[jax.ShapeDtypeStruct((length * tile, count * rows), jnp.float32) for length in pieces],
         scratch_shapes=[
             pltpu.VMEM((count * rows, width), jnp.bfloat16),
             pltpu.VMEM((chunks * tile, width), jnp.bfloat16),
@@ -127,16 +139,16 @@
 
 
 def statistics(near, near_other, far, far_other, diffs, mixing, late, parts):
-    vocabulary, rows = far.shape
+    vocabulary, rows = near.shape
     slots = diffs[0].shape[1]
     tile = tile_of(vocabulary)
     chunks = vocabulary // tile
-    pieces = len(near)
+    pieces = len(far)
     contract_last = (((1,), (1,)), ((), ()))
 
     def kernel(late_ref, *refs):
-        near_refs, near_other_refs, refs = refs[:pieces], refs[pieces : 2 * pieces], refs[2 * pieces :]
-        far_ref, far_other_ref, *refs = refs
+        near_ref, near_other_ref, *refs = refs
+        far_refs, far_other_refs, refs = refs[:pieces], refs[pieces : 2 * pieces], refs[2 * pieces :]
         diff_refs, mixing_refs, refs = refs[:2], refs[2:4], refs[4:]
         total_hbm, stats_ref, left, right, rows_in, mixed, left_sems, right_sems, out_sems, side_sems = refs
 
@@ -159,7 +171,7 @@
             every(left_side.shape[0] // tile, start)
 
         side_copies = [
-            pltpu.make_async_copy(source, into.at[n], side_sems.at[side, n])
+            pltpu.make_async_copy(source, into.at[:, pl.ds(n * slots, slots)], side_sems.at[side, n])
             for side, (sources, into) in enumerate(((mixing_refs, mixed), (diff_refs, rows_in)))
             for n, source in enumerate(sources)
         ]
@@ -168,27 +180,26 @@
 
         @pl.when(late_ref[0] == 0)
         def _():
+            start_all(0, near_ref, near_other_ref)
+
+        @pl.when(late_ref[0] == 1)
+        def _():
             first = 0
-            for left_side, right_side in zip(near_refs, near_other_refs):
+            for left_side, right_side in zip(far_refs, far_other_refs):
                 start_all(first, left_side, right_side)
                 first += left_side.shape[0] // tile
 
-        @pl.when(late_ref[0] == 1)
-        def _():
-            start_all(0, far_ref, far_other_ref)
-
         for copy in side_copies:
             copy.wait()
 
         def step(chunk, state):
-            for copy in fetch(chunk, chunk, far_ref, far_other_ref):
+            for copy in fetch(chunk, chunk, near_ref, near_other_ref):
                 copy.wait()
             place = rows_at(chunk, tile)
             total = left[place, :] + right[place, :]
-            for n in range(2):
-                total += lax.dot_general(
-                    rows_in[n, place, :], mixed[n], contract_last, preferred_element_type=jnp.float32
-                )
+            total += lax.dot_general(
+                rows_in[place, :], mixed[...], contract_last, preferred_element_type=jnp.float32
+            )
             left[place, :] = total
             out_copy(chunk).start()
             before, mass = state
@@ -211,15 +222,15 @@
             jax.ShapeDtypeStruct((parts, 2, rows), jnp.float32),
         ],
         scratch_shapes=[pltpu.VMEM((vocabulary, rows), jnp.float32)] * 2
-        + [pltpu.VMEM((2, vocabulary, slots), jnp.bfloat16), pltpu.VMEM((2, rows, slots), jnp.bfloat16)]
+        + [pltpu.VMEM((vocabulary, 2 * slots), jnp.bfloat16), pltpu.VMEM((rows, 2 * slots), jnp.bfloat16)]
         + [pltpu.SemaphoreType.DMA((chunks,))] * 3
         + [pltpu.SemaphoreType.DMA((2, 2))],
-        compiler_params=ROOM,
+        compiler_params=pltpu.CompilerParams(vmem_limit_bytes=12 * 2**20),
         cost_estimate=pl.CostEstimate(
             flops=4 * vocabulary * rows, bytes_accessed=16 * vocabulary * rows, transcendentals=vocabulary * rows
         ),
         name="statistics",
-    )(late.reshape(1), *near, *near_other, far, far_other, *diffs, *mixing)
+    )(late.reshape(1), in_hbm(near), in_hbm(near_other), *map(in_hbm, far), *far_other, *diffs, *mixing)
 
 
 def subtract(total, arrived):
@@ -262,7 +273,7 @@
         scratch_shapes=[pltpu.VMEM((vocabulary, rows), jnp.float32), pltpu.VMEM(arrived.shape, jnp.float32)]
         + [pltpu.SemaphoreType.DMA((chunks,))] * 2
         + [pltpu.SemaphoreType.DMA],
-        compiler_params=ROOM,
+        compiler_params=pltpu.CompilerParams(vmem_limit_bytes=12 * 2**20),
         cost_estimate=pl.CostEstimate(flops=vocabulary * rows, bytes_accessed=8 * vocabulary * rows, transcendentals=0),
         name="subtract",
     )(total, arrived)
@@ -286,8 +297,6 @@
     x0, y0, z1, z2 = move(own, 1), move(own, 2), move(own, 4), move(own, 8)
     slices = vocabulary_slices(after(diff_rows, own)[0, 0], parts)
 
-    own, x0, y0, z1, slices = lax.optimization_barrier((own, x0, y0, z1, slices))
-    x1, y1 = move(z1, 1), move(z1, 2)
     chosen = core * 8 * rows + jnp.arange(8 * rows, dtype=jnp.int32)
     factors = slot_factors(slot_code, slot_count)
 
@@ -298,15 +307,20 @@
 
     mixings = [mixing(core), mixing(1 - core)]
 
-    x1, y1, z2, y0, mixings = lax.optimization_barrier((x1, y1, z2, y0, mixings))
-    d0, d1, z3 = move(y0, 1), move(x1, 2), move(z2, 4)
-
-    d0, d1, z3, z2 = lax.optimization_barrier((d0, d1, z3, z2))
-    x2, y2, x3, y3 = move(z2, 1), move(z2, 2), move(z3, 1), move(z3, 2)
+    own, x0, y0, z1, slices, mixings = lax.optimization_barrier((own, x0, y0, z1, slices, mixings))
+    x1, y1, d0 = move(z1, 1), move(z1, 2), move(y0, 1)
+
+    x1, z2 = lax.optimization_barrier((x1, z2))
+    d1, z3 = move(x1, 2), move(z2, 4)
+
+    d0, y1, z2 = lax.optimization_barrier((d0, y1, z2))
+    x2, y2 = move(z2, 1), move(z2, 2)
+    d1, z3 = lax.optimization_barrier((d1, z3))
+    x3, y3 = move(z3, 1), move(z3, 2)
     first, half = me & 7, me // 8
     late = half ^ core
     chunks = weight_t.shape[0] // tile_of(weight_t.shape[0])
-    near = multiply([own, x0, y0, d0, z1, x1, y1, d1], weight_t, first, 0, chunks)
+    (near,) = multiply([own, x0, y0, d0, z1, x1, y1, d1], weight_t, first, [chunks])
 
     x3, y3, y2, x2, near, slices = lax.optimization_barrier((x3, y3, y2, x2, near, slices))
     d2, d3 = move(y2, 1), move(x3, 2)
@@ -314,12 +328,14 @@
     diffs = lax.all_to_all(slices, "wide", split_axis=0, concat_axis=0, tiled=True)
 
     d2, d3, near_other = lax.optimization_barrier((d2, d3, near_other))
-    far = multiply([z2, x2, y2, d2, z3, x3, y3, d3], weight_t, first, 0, chunks)
-    far, diffs = lax.optimization_barrier((far, diffs))
-    far_other = flip(far, "narrow", 1)
-    diffs = diffs.reshape(-1, weight_t.shape[0]).T
-    diffs_other = flip(diffs, "narrow", 1)
-    total, stats = statistics([near], [near_other], far, far_other, [diffs, diffs_other], mixings, late, parts)
+    middle = (chunks + 1) // 2
+    far = list(multiply([z2, x2, y2, d2, z3, x3, y3, d3], weight_t, first, [middle, chunks - middle]))
+    far_other = [flip(far[0], "narrow", 1)]
+    far[1], diffs = lax.optimization_barrier((far[1], diffs))
+    far_other.append(flip(far[1], "narrow", 1))
+    diffs = diffs.reshape(-1, weight_t.shape[0])
+    diffs, diffs_other = diffs.T, flip(diffs, "narrow", 1).T
+    total, stats = statistics(near, near_other, far, far_other, [diffs, diffs_other], mixings, late, parts)
     arrived = lax.all_to_all(stats, "wide", split_axis=0, concat_axis=0, tiled=True)
     return subtract(total, arrived).T
 

time: 94.8 us -> 91.5 us (0.965)
  waiting for transfers between devices: 20.4 us -> 14.9 us
  starting transfers between devices: 27 us -> 30.1 us
    ppermute x19 -> x20, waiting for transfers between devices: 17.3 us -> 12.5 us  [flip(): return lax.ppermute(a, axis, [(i, i ^ mask) for i in range(size)])]
    ppermute x19 -> x20, starting transfers between devices: 21.9 us -> 25.2 us  [flip(): return lax.ppermute(a, axis, [(i, i ^ mask) for i in range(size)])]
    unnamed x34 -> x30, local copies, waits for them, and re-layouts: 2.41 us -> 2.25 us
  transfers between devices with their start and end apart: 20 -> 21, of which waited for: 10 -> 8; matrix products, arithmetic and copies ran while one was open for 3% -> 3% of each run, Pallas kernels for 21% -> 22%
where the time goes in v3:
time: 91.5 us; the launch traced here: 91.1 us
  starting transfers between devices  30.1 us (33%)
  Pallas kernels  27.1 us (30%)
  waiting for transfers between devices  14.9 us (16%)
  blocking collectives  11.9 us (13%)
  local copies, waits for them, and re-layouts  3.94 us (4%)
  other arithmetic  3.01 us (3%)
    ppermute x20, starting transfers between devices, flip(): return lax.ppermute(a, axis, [(i, i ^ mask) for i in range(size)])  25.2 us
    pallas_call x2, Pallas kernels, multiply(): pl.pallas_call(kernel, in_specs=[SCALAR] + [ANYWHERE] * (count + 1), out_...  18.2 us
    ppermute x20, waiting for transfers between devices, flip(): return lax.ppermute(a, axis, [(i, i ^ mask) for i in range(size)])  12.5 us
    all_to_all x1, blocking collectives, body(): lax.all_to_all(stats, 'wide', split_axis=0, concat_axis=0, tiled=True)  11.9 us
    all_to_all x1, starting transfers between devices, body(): lax.all_to_all(slices, 'wide', split_axis=0, concat_axis=0, tiled=True)  4.87 us
    pallas_call x1, Pallas kernels, statistics(): pl.pallas_call(kernel, in_specs=[SCALAR] + [ANYWHERE] * (2 * pieces + 6),...  4.31 us
    pallas_call x1, Pallas kernels, subtract(): pl.pallas_call(kernel, in_specs=[ANYWHERE] * 2, out_specs=ANYWHERE, out_s...  2.54 us
    all_to_all x1, waiting for transfers between devices, body(): lax.all_to_all(slices, 'wide', split_axis=0, concat_axis=0, tiled=True)  2.48 us
  transfers between devices with their start and end apart: 21, of which 8 were waited for; matrix products, arithmetic and copies ran while one was open for 3% of the time, Pallas kernels for 22%

profile of v3, /device:TPU:0, one launch (start us, length us, event | category | flops | bytes accessed | tf_op | source)
XLA Modules:
  0.0 91.1 jit_solution(17372432614213621076)
XLA Ops:
  4.1 2.7 %collective-permute-start.3 = (bf16[32,4096]{1,0:T(8,128)(2,1)S(1)}, bf16[32,4096]{1,0:T(8,128)(2,1)S(1)}, u32[]{:S(2)}, u32[]{:S(2)}) collective-permute-start(bf16[32,4096]{1,0:T(8,128)(2,1)S(1)} %fusion.2.refs_0_), channel_id=1, source_target_pairs={{0,8},{2,10},{4,12},{6,14},{8,0},{10,2},{12,4},{14,6},{16,24},{18,... | collective-permute-start | bytes 786440 | tf_op jit(solution)/shard_map/ppermute | solution.py:19
  6.8 1.5 %collective-permute-start.2 = (bf16[32,4096]{1,0:T(8,128)(2,1)S(1)}, bf16[32,4096]{1,0:T(8,128)(2,1)S(1)}, u32[]{:S(2)}, u32[]{:S(2)}) collective-permute-start(bf16[32,4096]{1,0:T(8,128)(2,1)S(1)} %fusion.2.refs_0_), channel_id=1, source_target_pairs={{0,4},{2,6},{4,0},{6,2},{8,12},{10,14},{12,8},{14,10},{16,20},{18,... | collective-permute-start | bytes 786440 | tf_op jit(solution)/shard_map/ppermute | solution.py:19
  8.3 1.5 %collective-permute-start.1 = (bf16[32,4096]{1,0:T(8,128)(2,1)S(1)}, bf16[32,4096]{1,0:T(8,128)(2,1)S(1)}, u32[]{:S(2)}, u32[]{:S(2)}) collective-permute-start(bf16[32,4096]{1,0:T(8,128)(2,1)S(1)} %fusion.2.refs_0_), channel_id=1, source_target_pairs={{0,2},{2,0},{4,6},{6,4},{8,10},{10,8},{12,14},{14,12},{16,18},{18,... | collective-permute-start | bytes 786440 | tf_op jit(solution)/shard_map/ppermute | solution.py:19
  10.6 2.7 %collective-permute-start.5 = (bf16[32,4096]{1,0:T(8,128)(2,1)S(1)}, bf16[32,4096]{1,0:T(8,128)(2,1)S(1)}, u32[]{:S(2)}, u32[]{:S(2)}) collective-permute-start(bf16[32,4096]{1,0:T(8,128)(2,1)S(1)} %fusion.2.refs_0_), channel_id=1, source_target_pairs={{0,16},{2,18},{4,20},{6,22},{8,24},{10,26},{12,28},{14,30},{16,0},... | collective-permute-start | bytes 786440 | tf_op jit(solution)/shard_map/ppermute | solution.py:19
  13.3 2.0 %vocabulary_slices.1 = bf16[16,8,2000]{2,1,0:T(8,128)(2,1)} custom-call(bf16[8,32000]{1,0:T(8,128)(2,1)} %bitcast.19), custom_call_target="tpu_custom_call" | custom-call | bytes 1024000 | tf_op jit(solution)/shard_map/vocabulary_slices/pallas_call | solution.py:41
  15.3 1.1 %collective-permute-done.1.refs_1_ = bf16[32,4096]{1,0:T(8,128)(2,1)S(1)} collective-permute-done((bf16[32,4096]{1,0:T(8,128)(2,1)S(1)}, bf16[32,4096]{1,0:T(8,128)(2,1)S(1)}, u32[]{:S(2)}, u32[]{:S(2)}) %collective-permute-start.1) | collective-permute-done | bytes 262176 | tf_op jit(solution)/shard_map/ppermute | solution.py:19
  16.5 2.2 %collective-permute-start.4 = (bf16[32,4096]{1,0:T(8,128)(2,1)S(1)}, bf16[32,4096]{1,0:T(8,128)(2,1)S(1)}, u32[]{:S(2)}, u32[]{:S(2)}) collective-permute-start(bf16[32,4096]{1,0:T(8,128)(2,1)S(1)} %collective-permute-done.3.refs_4_), channel_id=1, source_target_pairs={{0,2},{2,0},{4,6},{6,4},{8,10},{10,8},{12,14},{14,12},{16,18},{18,... | collective-permute-start | bytes 786440 | tf_op jit(solution)/shard_map/ppermute | solution.py:19
  18.6 2.5 %collective-permute-start.11 = (bf16[32,4096]{1,0:T(8,128)(2,1)S(1)}, bf16[32,4096]{1,0:T(8,128)(2,1)S(1)}, u32[]{:S(2)}, u32[]{:S(2)}) collective-permute-start(bf16[32,4096]{1,0:T(8,128)(2,1)S(1)} %collective-permute-done.3.refs_4_), channel_id=1, source_target_pairs={{0,4},{2,6},{4,0},{6,2},{8,12},{10,14},{12,8},{14,10},{16,20},{18,... | collective-permute-start | bytes 786440 | tf_op jit(solution)/shard_map/ppermute | solution.py:19
  21.2 3.8 %collective-permute-done.5.refs_0_ = bf16[32,4096]{1,0:T(8,128)(2,1)S(1)} collective-permute-done((bf16[32,4096]{1,0:T(8,128)(2,1)S(1)}, bf16[32,4096]{1,0:T(8,128)(2,1)S(1)}, u32[]{:S(2)}, u32[]{:S(2)}) %collective-permute-start.5) | collective-permute-done | bytes 262176 | tf_op jit(solution)/shard_map/ppermute | solution.py:19
  25.8 2.5 %collective-permute-start.6 = (bf16[32,4096]{1,0:T(8,128)(2,1)S(1)}, bf16[32,4096]{1,0:T(8,128)(2,1)S(1)}, u32[]{:S(2)}, u32[]{:S(2)}) collective-permute-start(bf16[32,4096]{1,0:T(8,128)(2,1)S(1)} %collective-permute-done.4.refs_5_), channel_id=1, source_target_pairs={{0,4},{2,6},{4,0},{6,2},{8,12},{10,14},{12,8},{14,10},{16,20},{18,... | collective-permute-start | bytes 786440 | tf_op jit(solution)/shard_map/ppermute | solution.py:19
  28.3 2.1 %collective-permute-done.10.refs_3_ = bf16[32,4096]{1,0:T(8,128)(2,1)S(1)} collective-permute-done((bf16[32,4096]{1,0:T(8,128)(2,1)S(1)}, bf16[32,4096]{1,0:T(8,128)(2,1)S(1)}, u32[]{:S(2)}, u32[]{:S(2)}) %collective-permute-start.10) | collective-permute-done | bytes 262176 | tf_op jit(solution)/shard_map/ppermute | solution.py:19
  30.4 1.8 %collective-permute-start.13 = (bf16[32,4096]{1,0:T(8,128)(2,1)S(1)}, bf16[32,4096]{1,0:T(8,128)(2,1)S(1)}, u32[]{:S(2)}, u32[]{:S(2)}) collective-permute-start(bf16[32,4096]{1,0:T(8,128)(2,1)S(1)} %collective-permute-done.5.refs_0_), channel_id=1, source_target_pairs={{0,2},{2,0},{4,6},{6,4},{8,10},{10,8},{12,14},{14,12},{16,18},{18,... | collective-permute-start | bytes 786440 | tf_op jit(solution)/shard_map/ppermute | solution.py:19
  32.2 2.5 %collective-permute-start.12 = (bf16[32,4096]{1,0:T(8,128)(2,1)S(1)}, bf16[32,4096]{1,0:T(8,128)(2,1)}, u32[]{:S(2)}, u32[]{:S(2)}) collective-permute-start(bf16[32,4096]{1,0:T(8,128)(2,1)S(1)} %collective-permute-done.5.refs_0_), channel_id=1, source_target_pairs={{0,4},{2,6},{4,0},{6,2},{8,12},{10,14},{12,8},{14,10},{16,20},{18,... | collective-permute-start | bytes 786440 | tf_op jit(solution)/shard_map/ppermute | solution.py:19
  35.5 2.1 %collective-permute-start.8 = (bf16[32,4096]{1,0:T(8,128)(2,1)S(1)}, bf16[32,4096]{1,0:T(8,128)(2,1)}, u32[]{:S(2)}, u32[]{:S(2)}) collective-permute-start(bf16[32,4096]{1,0:T(8,128)(2,1)S(1)} %collective-permute-done.7.refs_4_), channel_id=1, source_target_pairs={{0,2},{2,0},{4,6},{6,4},{8,10},{10,8},{12,14},{14,12},{16,18},{18,... | collective-permute-start | bytes 786440 | tf_op jit(solution)/shard_map/ppermute | solution.py:19
  37.7 8.7 %multiply.5.refs_0_ = f32[2000,256]{1,0:T(8,128)} custom-call(s32[1]{0:T(128)} %bitcast.2.first_ref, bf16[32,4096]{1,0:T(8,128)(2,1)} %copy-done.1, bf16[32,4096]{1,0:T(8,128)(2,1)} %copy-done.5, bf16[32,4096]{1,0:T(8,128)(2,1)} %copy-done.4, bf16[32,4096]{1,0:T(8,128)(2,1)} %copy-done.11, bf16[32,4096]{1,0:T(8,128)(2,1)} %copy-done.3, ...), custom_call_target="tpu_custom_call" | custom-call | flops 16777216000 | bytes 65536000 | tf_op jit(solution)/shard_map/multiply/pallas_call | solution.py:120
  47.3 1.9 %collective-permute-start.15 = (bf16[32,4096]{1,0:T(8,128)(2,1)}, bf16[32,4096]{1,0:T(8,128)(2,1)S(1)}, u32[]{:S(2)}, u32[]{:S(2)}) collective-permute-start(bf16[32,4096]{1,0:T(8,128)(2,1)} %collective-permute-done.8.refs_5_), channel_id=1, source_target_pairs={{0,4},{2,6},{4,0},{6,2},{8,12},{10,14},{12,8},{14,10},{16,20},{18,... | collective-permute-start | bytes 786440 | tf_op jit(solution)/shard_map/ppermute | solution.py:19
  49.2 4.9 %all-to-all-start = ((bf16[16,8,2000]{2,1,0:T(8,128)(2,1)}), bf16[16,8,2000]{2,1,0:T(8,128)(2,1)S(1)}, u32[]{:S(2)}, u32[]{:S(2)}) async-start(bf16[16,8,2000]{2,1,0:T(8,128)(2,1)} %vocabulary_slices.1), calls=%async_computation | async-start | bytes 1048576 | tf_op jit(solution)/shard_map/all_to_all | solution.py:328
  54.1 2.1 %collective-permute-done.14.refs_3_ = bf16[32,4096]{1,0:T(8,128)(2,1)S(1)} collective-permute-done((bf16[32,4096]{1,0:T(8,128)(2,1)}, bf16[32,4096]{1,0:T(8,128)(2,1)S(1)}, u32[]{:S(2)}, u32[]{:S(2)}) %collective-permute-start.14) | collective-permute-done | bytes 262176 | tf_op jit(solution)/shard_map/ppermute | solution.py:19
  57.3 9.4 %multiply.6 = (f32[1200,256]{1,0:T(8,128)}, f32[800,256]{1,0:T(8,128)}) custom-call(s32[1]{0:T(128)} %bitcast.2.first_ref, bf16[32,4096]{1,0:T(8,128)(2,1)} %copy-done.2, bf16[32,4096]{1,0:T(8,128)(2,1)} %copy-done.7, bf16[32,4096]{1,0:T(8,128)(2,1)} %collective-permute-done.12.refs_2_, bf16[32,4096]{1,0:T(8,128)(2,1)} %copy-done.13, ...), custom_call_target="tpu_custom_call" | custom-call | flops 16777216000 | bytes 65536000 | tf_op jit(solution)/shard_map/multiply/pallas_call | solution.py:120
  66.8 2.5 %all-to-all-done = bf16[16,8,2000]{2,1,0:T(8,128)(2,1)S(1)} async-done(((bf16[16,8,2000]{2,1,0:T(8,128)(2,1)}), bf16[16,8,2000]{2,1,0:T(8,128)(2,1)S(1)}, u32[]{:S(2)}, u32[]{:S(2)}) %all-to-all-start) | async-done | bytes 512032 | tf_op jit(solution)/shard_map/all_to_all | solution.py:328
  70.2 2.2 %collective-permute-done.19 = bf16[128,2000]{0,1:T(8,128)(2,1)S(1)} collective-permute-done((bf16[128,2000]{0,1:T(8,128)(2,1)S(1)}, bf16[128,2000]{0,1:T(8,128)(2,1)S(1)}, u32[]{:S(2)}, u32[]{:S(2)}) %collective-permute-start.19) | collective-permute-done | bytes 512032 | tf_op jit(solution)/shard_map/ppermute | solution.py:19
  72.4 4.3 %statistics.1 = (f32[2000,256]{1,0:T(8,128)S(1)}, f32[16,2,256]{2,1,0:T(2,128)S(1)}) custom-call(s32[1]{0:T(128)} %bitcast.late_ref, f32[2000,256]{1,0:T(8,128)} %multiply.5.refs_0_, f32[2000,256]{1,0:T(8,128)} %copy-done, f32[1200,256]{1,0:T(8,128)} %get-tuple-element.56.refs_2_, f32[800,256]{1,0:T(8,128)} %get-tuple-element.59.refs_3_, ...), custom_call_target="tpu_custom_call" | custom-call | flops 2048000 | bytes 8192000 | tf_op jit(solution)/shard_map/statistics/pallas_call | solution.py:216
  76.7 11.9 %all_to_all.10.arrived_hbm = f32[16,2,256]{2,1,0:T(2,128)S(1)} all-to-all(f32[16,2,256]{2,1,0:T(2,128)S(1)} %get-tuple-element.64), channel_id=1, replica_groups=mesh['wide'=16,'narrow'=2] {'wide'}, dimensions={0} | all-to-all | bytes 65536 | tf_op jit(solution)/shard_map/all_to_all | solution.py:339
  88.6 2.5 %subtract.2 = f32[2000,256]{1,0:T(8,128)} custom-call(f32[2000,256]{1,0:T(8,128)S(1)} %get-tuple-element.63.total_hbm, f32[16,2,256]{2,1,0:T(2,128)S(1)} %all_to_all.10.arrived_hbm), custom_call_target="tpu_custom_call" | custom-call | flops 512000 | bytes 4096000 | tf_op jit(solution)/shard_map/subtract/pallas_call | solution.py:268
  (71 shorter events, 9.3 us)
Async XLA Ops:
  1.1 1.9 %collective-permute-start = (f32[32]{0:T(128)S(1)}, f32[32]{0:T(128)S(1)}, u32[]{:S(2)}, u32[]{:S(2)}) collective-permute-start(f32[32]{0:T(128)S(1)} %fusion), channel_id=1, source_target_pairs={{0,1},{1,0},{2,3},{3,2},{4,5},{5,4},{6,7},{7,6},{8,9},{9,8},{10,11... | collective-permute-start | bytes 392 | tf_op jit(solution)/shard_map/ppermute | solution.py:19
  4.1 33.5 %copy-start.1 = (bf16[32,4096]{1,0:T(8,128)(2,1)}, bf16[32,4096]{1,0:T(8,128)(2,1)S(1)}, u32[]{:S(2)}) copy-start(bf16[32,4096]{1,0:T(8,128)(2,1)S(1)} %fusion.2.refs_0_) | copy-start | bytes 786436
  4.1 11.2 %collective-permute-start.3 = (bf16[32,4096]{1,0:T(8,128)(2,1)S(1)}, bf16[32,4096]{1,0:T(8,128)(2,1)S(1)}, u32[]{:S(2)}, u32[]{:S(2)}) collective-permute-start(bf16[32,4096]{1,0:T(8,128)(2,1)S(1)} %fusion.2.refs_0_), channel_id=1, source_target_pairs={{0,8},{2,10},{4,12},{6,14},{8,0},{10,2},{12,4},{14,6},{16,24},{18,... | collective-permute-start | bytes 786440 | tf_op jit(solution)/shard_map/ppermute | solution.py:19
  6.8 8.5 %collective-permute-start.2 = (bf16[32,4096]{1,0:T(8,128)(2,1)S(1)}, bf16[32,4096]{1,0:T(8,128)(2,1)S(1)}, u32[]{:S(2)}, u32[]{:S(2)}) collective-permute-start(bf16[32,4096]{1,0:T(8,128)(2,1)S(1)} %fusion.2.refs_0_), channel_id=1, source_target_pairs={{0,4},{2,6},{4,0},{6,2},{8,12},{10,14},{12,8},{14,10},{16,20},{18,... | collective-permute-start | bytes 786440 | tf_op jit(solution)/shard_map/ppermute | solution.py:19
  8.3 8.1 %collective-permute-start.1 = (bf16[32,4096]{1,0:T(8,128)(2,1)S(1)}, bf16[32,4096]{1,0:T(8,128)(2,1)S(1)}, u32[]{:S(2)}, u32[]{:S(2)}) collective-permute-start(bf16[32,4096]{1,0:T(8,128)(2,1)S(1)} %fusion.2.refs_0_), channel_id=1, source_target_pairs={{0,2},{2,0},{4,6},{6,4},{8,10},{10,8},{12,14},{14,12},{16,18},{18,... | collective-permute-start | bytes 786440 | tf_op jit(solution)/shard_map/ppermute | solution.py:19
  10.6 14.4 %collective-permute-start.5 = (bf16[32,4096]{1,0:T(8,128)(2,1)S(1)}, bf16[32,4096]{1,0:T(8,128)(2,1)S(1)}, u32[]{:S(2)}, u32[]{:S(2)}) collective-permute-start(bf16[32,4096]{1,0:T(8,128)(2,1)S(1)} %fusion.2.refs_0_), channel_id=1, source_target_pairs={{0,16},{2,18},{4,20},{6,22},{8,24},{10,26},{12,28},{14,30},{16,0},... | collective-permute-start | bytes 786440 | tf_op jit(solution)/shard_map/ppermute | solution.py:19
  15.3 22.3 %copy-start.3 = (bf16[32,4096]{1,0:T(8,128)(2,1)}, bf16[32,4096]{1,0:T(8,128)(2,1)S(1)}, u32[]{:S(2)}) copy-start(bf16[32,4096]{1,0:T(8,128)(2,1)S(1)} %collective-permute-done.3.refs_4_) | copy-start | bytes 786436
  15.3 22.3 %copy-start.4 = (bf16[32,4096]{1,0:T(8,128)(2,1)}, bf16[32,4096]{1,0:T(8,128)(2,1)S(1)}, u32[]{:S(2)}) copy-start(bf16[32,4096]{1,0:T(8,128)(2,1)S(1)} %collective-permute-done.2.refs_2_) | copy-start | bytes 786436
  16.5 9.3 %collective-permute-start.4 = (bf16[32,4096]{1,0:T(8,128)(2,1)S(1)}, bf16[32,4096]{1,0:T(8,128)(2,1)S(1)}, u32[]{:S(2)}, u32[]{:S(2)}) collective-permute-start(bf16[32,4096]{1,0:T(8,128)(2,1)S(1)} %collective-permute-done.3.refs_4_), channel_id=1, source_target_pairs={{0,2},{2,0},{4,6},{6,4},{8,10},{10,8},{12,14},{14,12},{16,18},{18,... | collective-permute-start | bytes 786440 | tf_op jit(solution)/shard_map/ppermute | solution.py:19
  18.6 11.8 %collective-permute-start.11 = (bf16[32,4096]{1,0:T(8,128)(2,1)S(1)}, bf16[32,4096]{1,0:T(8,128)(2,1)S(1)}, u32[]{:S(2)}, u32[]{:S(2)}) collective-permute-start(bf16[32,4096]{1,0:T(8,128)(2,1)S(1)} %collective-permute-done.3.refs_4_), channel_id=1, source_target_pairs={{0,4},{2,6},{4,0},{6,2},{8,12},{10,14},{12,8},{14,10},{16,20},{18,... | collective-permute-start | bytes 786440 | tf_op jit(solution)/shard_map/ppermute | solution.py:19
  21.2 9.3 %collective-permute-start.10 = (bf16[32,4096]{1,0:T(8,128)(2,1)S(1)}, bf16[32,4096]{1,0:T(8,128)(2,1)S(1)}, u32[]{:S(2)}, u32[]{:S(2)}) collective-permute-start(bf16[32,4096]{1,0:T(8,128)(2,1)S(1)} %collective-permute-done.2.refs_2_), channel_id=1, source_target_pairs={{0,2},{2,0},{4,6},{6,4},{8,10},{10,8},{12,14},{14,12},{16,18},{18,... | collective-permute-start | bytes 786440 | tf_op jit(solution)/shard_map/ppermute | solution.py:19
  25.8 9.0 %collective-permute-start.6 = (bf16[32,4096]{1,0:T(8,128)(2,1)S(1)}, bf16[32,4096]{1,0:T(8,128)(2,1)S(1)}, u32[]{:S(2)}, u32[]{:S(2)}) collective-permute-start(bf16[32,4096]{1,0:T(8,128)(2,1)S(1)} %collective-permute-done.4.refs_5_), channel_id=1, source_target_pairs={{0,4},{2,6},{4,0},{6,2},{8,12},{10,14},{12,8},{14,10},{16,20},{18,... | collective-permute-start | bytes 786440 | tf_op jit(solution)/shard_map/ppermute | solution.py:19
  28.3 7.2 %collective-permute-start.7 = (bf16[32,4096]{1,0:T(8,128)(2,1)S(1)}, bf16[32,4096]{1,0:T(8,128)(2,1)S(1)}, u32[]{:S(2)}, u32[]{:S(2)}) collective-permute-start(bf16[32,4096]{1,0:T(8,128)(2,1)S(1)} %collective-permute-done.5.refs_0_), channel_id=1, source_target_pairs={{0,8},{2,10},{4,12},{6,14},{8,0},{10,2},{12,4},{14,6},{16,24},{18,... | collective-permute-start | bytes 786440 | tf_op jit(solution)/shard_map/ppermute | solution.py:19
  30.4 16.0 %collective-permute-start.13 = (bf16[32,4096]{1,0:T(8,128)(2,1)S(1)}, bf16[32,4096]{1,0:T(8,128)(2,1)S(1)}, u32[]{:S(2)}, u32[]{:S(2)}) collective-permute-start(bf16[32,4096]{1,0:T(8,128)(2,1)S(1)} %collective-permute-done.5.refs_0_), channel_id=1, source_target_pairs={{0,2},{2,0},{4,6},{6,4},{8,10},{10,8},{12,14},{14,12},{16,18},{18,... | collective-permute-start | bytes 786440 | tf_op jit(solution)/shard_map/ppermute | solution.py:19
  32.2 14.2 %collective-permute-start.12 = (bf16[32,4096]{1,0:T(8,128)(2,1)S(1)}, bf16[32,4096]{1,0:T(8,128)(2,1)}, u32[]{:S(2)}, u32[]{:S(2)}) collective-permute-start(bf16[32,4096]{1,0:T(8,128)(2,1)S(1)} %collective-permute-done.5.refs_0_), channel_id=1, source_target_pairs={{0,4},{2,6},{4,0},{6,2},{8,12},{10,14},{12,8},{14,10},{16,20},{18,... | collective-permute-start | bytes 786440 | tf_op jit(solution)/shard_map/ppermute | solution.py:19
  35.5 11.0 %collective-permute-start.9 = (bf16[32,4096]{1,0:T(8,128)(2,1)S(1)}, bf16[32,4096]{1,0:T(8,128)(2,1)S(1)}, u32[]{:S(2)}, u32[]{:S(2)}) collective-permute-start(bf16[32,4096]{1,0:T(8,128)(2,1)S(1)} %collective-permute-done.7.refs_4_), channel_id=1, source_target_pairs={{0,4},{2,6},{4,0},{6,2},{8,12},{10,14},{12,8},{14,10},{16,20},{18,... | collective-permute-start | bytes 786440 | tf_op jit(solution)/shard_map/ppermute | solution.py:19
  35.5 11.8 %collective-permute-start.8 = (bf16[32,4096]{1,0:T(8,128)(2,1)S(1)}, bf16[32,4096]{1,0:T(8,128)(2,1)}, u32[]{:S(2)}, u32[]{:S(2)}) collective-permute-start(bf16[32,4096]{1,0:T(8,128)(2,1)S(1)} %collective-permute-done.7.refs_4_), channel_id=1, source_target_pairs={{0,2},{2,0},{4,6},{6,4},{8,10},{10,8},{12,14},{14,12},{16,18},{18,... | collective-permute-start | bytes 786440 | tf_op jit(solution)/shard_map/ppermute | solution.py:19
  47.3 9.3 %collective-permute-start.16 = (f32[2000,256]{1,0:T(8,128)}, f32[2000,256]{1,0:T(8,128)S(1)}, u32[]{:S(2)}, u32[]{:S(2)}) collective-permute-start(f32[2000,256]{1,0:T(8,128)} %multiply.5.refs_0_), channel_id=1, source_target_pairs={{0,1},{1,0},{2,3},{3,2},{4,5},{5,4},{6,7},{7,6},{8,9},{9,8},{10,11... | collective-permute-start | bytes 6144008 | tf_op jit(solution)/shard_map/ppermute | solution.py:19
  47.3 8.9 %collective-permute-start.14 = (bf16[32,4096]{1,0:T(8,128)(2,1)}, bf16[32,4096]{1,0:T(8,128)(2,1)S(1)}, u32[]{:S(2)}, u32[]{:S(2)}) collective-permute-start(bf16[32,4096]{1,0:T(8,128)(2,1)} %collective-permute-done.12.refs_2_), channel_id=1, source_target_pairs={{0,2},{2,0},{4,6},{6,4},{8,10},{10,8},{12,14},{14,12},{16,18},{18,... | collective-permute-start | bytes 786440 | tf_op jit(solution)/shard_map/ppermute | solution.py:19
  47.3 9.3 %collective-permute-start.15 = (bf16[32,4096]{1,0:T(8,128)(2,1)}, bf16[32,4096]{1,0:T(8,128)(2,1)S(1)}, u32[]{:S(2)}, u32[]{:S(2)}) collective-permute-start(bf16[32,4096]{1,0:T(8,128)(2,1)} %collective-permute-done.8.refs_5_), channel_id=1, source_target_pairs={{0,4},{2,6},{4,0},{6,2},{8,12},{10,14},{12,8},{14,10},{16,20},{18,... | collective-permute-start | bytes 786440 | tf_op jit(solution)/shard_map/ppermute | solution.py:19
  49.2 20.1 %all-to-all-start = ((bf16[16,8,2000]{2,1,0:T(8,128)(2,1)}), bf16[16,8,2000]{2,1,0:T(8,128)(2,1)S(1)}, u32[]{:S(2)}, u32[]{:S(2)}) async-start(bf16[16,8,2000]{2,1,0:T(8,128)(2,1)} %vocabulary_slices.1), calls=%async_computation | async-start | bytes 1048576 | tf_op jit(solution)/shard_map/all_to_all | solution.py:328
  66.7 5.6 %collective-permute-start.17 = (f32[1200,256]{1,0:T(8,128)}, f32[1200,256]{1,0:T(8,128)S(1)}, u32[]{:S(2)}, u32[]{:S(2)}) collective-permute-start(f32[1200,256]{1,0:T(8,128)} %get-tuple-element.56.refs_2_), channel_id=1, source_target_pairs={{0,1},{1,0},{2,3},{3,2},{4,5},{5,4},{6,7},{7,6},{8,9},{9,8},{10,11... | collective-permute-start | bytes 3686408 | tf_op jit(solution)/shard_map/ppermute | solution.py:19
  69.3 3.1 %collective-permute-start.18 = (f32[800,256]{1,0:T(8,128)}, f32[800,256]{1,0:T(8,128)S(1)}, u32[]{:S(2)}, u32[]{:S(2)}) collective-permute-start(f32[800,256]{1,0:T(8,128)} %get-tuple-element.59.refs_3_), channel_id=1, source_target_pairs={{0,1},{1,0},{2,3},{3,2},{4,5},{5,4},{6,7},{7,6},{8,9},{9,8},{10,11... | collective-permute-start | bytes 2457608 | tf_op jit(solution)/shard_map/ppermute | solution.py:19
  69.6 2.8 %collective-permute-start.19 = (bf16[128,2000]{0,1:T(8,128)(2,1)S(1)}, bf16[128,2000]{0,1:T(8,128)(2,1)S(1)}, u32[]{:S(2)}, u32[]{:S(2)}) collective-permute-start(bf16[128,2000]{0,1:T(8,128)(2,1)S(1)} %copy.17), channel_id=1, source_target_pairs={{0,1},{1,0},{2,3},{3,2},{4,5},{5,4},{6,7},{7,6},{8,9},{9,8},{10,11... | collective-permute-start | bytes 1536008 | tf_op jit(solution)/shard_map/ppermute | solution.py:19
  (12 other events, 94.9 us)

commit v4 on v3

--- a/solution.py
+++ b/solution.py
@@ -11,7 +11,7 @@
 epsilon = 1e-05
 ANYWHERE = pl.BlockSpec(memory_space=pl.ANY)
 SCALAR = pl.BlockSpec(memory_space=pltpu.SMEM)
-ROOM = pltpu.CompilerParams(vmem_limit_bytes=56 * 2**20)
+ROOM = pltpu.CompilerParams(vmem_limit_bytes=46 * 2**20)
 
 
 def flip(a, axis, mask):
@@ -66,7 +66,7 @@
     return pl.ds(pl.multiple_of(i * tile, 8), tile)
 
 
-def multiply(blocks, weight_t, first, pieces):
+def multiply(blocks, fresh, weight_t, first, pieces):
     width = weight_t.shape[1]
     count, rows = len(blocks), blocks[0].shape[0]
     tile = tile_of(weight_t.shape[0])
@@ -135,7 +135,7 @@
             flops=8 * chunks * tile * width * count * rows, bytes_accessed=8 * chunks * tile * width, transcendentals=0
         ),
         name="multiply",
-    )(first.reshape(1), *blocks, weight_t)
+    )(first.reshape(1), *(a if n in fresh else in_hbm(a) for n, a in enumerate(blocks)), in_hbm(weight_t))
 
 
 def statistics(near, near_other, far, far_other, diffs, mixing, late, parts):
@@ -320,7 +320,7 @@
     first, half = me & 7, me // 8
     late = half ^ core
     chunks = weight_t.shape[0] // tile_of(weight_t.shape[0])
-    (near,) = multiply([own, x0, y0, d0, z1, x1, y1, d1], weight_t, first, [chunks])
+    (near,) = multiply([own, x0, y0, d0, z1, x1, y1, d1], [7], weight_t, first, [chunks])
 
     x3, y3, y2, x2, near, slices = lax.optimization_barrier((x3, y3, y2, x2, near, slices))
     d2, d3 = move(y2, 1), move(x3, 2)
@@ -329,7 +329,7 @@
 
     d2, d3, near_other = lax.optimization_barrier((d2, d3, near_other))
     middle = (chunks + 1) // 2
-    far = list(multiply([z2, x2, y2, d2, z3, x3, y3, d3], weight_t, first, [middle, chunks - middle]))
+    far = list(multiply([z2, x2, y2, d2, z3, x3, y3, d3], [3, 7], weight_t, first, [middle, chunks - middle]))
     far_other = [flip(far[0], "narrow", 1)]
     far[1], diffs = lax.optimization_barrier((far[1], diffs))
     far_other.append(flip(far[1], "narrow", 1))

time: 91.5 us -> 91.1 us (level)
  local copies, waits for them, and re-layouts: 3.94 us -> 5.11 us
    ppermute x20, waiting for transfers between devices: 12.5 us -> 10.7 us  [flip(): return lax.ppermute(a, axis, [(i, i ^ mask) for i in range(size)])]
    reshape x1, local copies, waits for them, and re-layouts: 0.3 us -> 1.33 us  [body(): diffs = diffs.reshape(-1, weight_t.shape[0])]
    unnamed x30 -> x28, local copies, waits for them, and re-layouts: 2.25 us -> 2.38 us
  transfers between devices with their start and end apart: 21 -> 21, of which waited for: 8 -> 8; matrix products, arithmetic and copies ran while one was open for 3% -> 4% of each run, Pallas kernels for 22% -> 21%
where the time goes in v4:
time: 91.1 us; the launch traced here: 90.6 us
  starting transfers between devices  30.6 us (34%)
  Pallas kernels  26.2 us (29%)
  waiting for transfers between devices  14.1 us (15%)
  blocking collectives  11.4 us (13%)
  local copies, waits for them, and re-layouts  5.11 us (6%)
  other arithmetic  3.01 us (3%)
    ppermute x20, starting transfers between devices, flip(): return lax.ppermute(a, axis, [(i, i ^ mask) for i in range(size)])  25.3 us
    pallas_call x2, Pallas kernels, multiply(): pl.pallas_call(kernel, in_specs=[SCALAR] + [ANYWHERE] * (count + 1), out_...  17.3 us
    all_to_all x1, blocking collectives, body(): lax.all_to_all(stats, 'wide', split_axis=0, concat_axis=0, tiled=True)  11.4 us
    ppermute x20, waiting for transfers between devices, flip(): return lax.ppermute(a, axis, [(i, i ^ mask) for i in range(size)])  10.7 us
    all_to_all x1, starting transfers between devices, body(): lax.all_to_all(slices, 'wide', split_axis=0, concat_axis=0, tiled=True)  5.27 us
    pallas_call x1, Pallas kernels, statistics(): pl.pallas_call(kernel, in_specs=[SCALAR] + [ANYWHERE] * (2 * pieces + 6),...  4.33 us
    all_to_all x1, waiting for transfers between devices, body(): lax.all_to_all(slices, 'wide', split_axis=0, concat_axis=0, tiled=True)  3.36 us
    pallas_call x1, Pallas kernels, subtract(): pl.pallas_call(kernel, in_specs=[ANYWHERE] * 2, out_specs=ANYWHERE, out_s...  2.54 us
  transfers between devices with their start and end apart: 21, of which 8 were waited for; matrix products, arithmetic and copies ran while one was open for 4% of the time, Pallas kernels for 21%

profile of v4, /device:TPU:0, one launch (start us, length us, event | category | flops | bytes accessed | tf_op | source)
XLA Modules:
  0.0 90.6 jit_solution(17971583111498624522)
XLA Ops:
  4.1 2.7 %collective-permute-start.3 = (bf16[32,4096]{1,0:T(8,128)(2,1)S(1)}, bf16[32,4096]{1,0:T(8,128)(2,1)S(1)}, u32[]{:S(2)}, u32[]{:S(2)}) collective-permute-start(bf16[32,4096]{1,0:T(8,128)(2,1)S(1)} %fusion.2.refs_0_), channel_id=1, source_target_pairs={{0,8},{2,10},{4,12},{6,14},{8,0},{10,2},{12,4},{14,6},{16,24},{18,... | collective-permute-start | bytes 786440 | tf_op jit(solution)/shard_map/ppermute | solution.py:19
  6.8 1.5 %collective-permute-start.2 = (bf16[32,4096]{1,0:T(8,128)(2,1)S(1)}, bf16[32,4096]{1,0:T(8,128)(2,1)S(1)}, u32[]{:S(2)}, u32[]{:S(2)}) collective-permute-start(bf16[32,4096]{1,0:T(8,128)(2,1)S(1)} %fusion.2.refs_0_), channel_id=1, source_target_pairs={{0,4},{2,6},{4,0},{6,2},{8,12},{10,14},{12,8},{14,10},{16,20},{18,... | collective-permute-start | bytes 786440 | tf_op jit(solution)/shard_map/ppermute | solution.py:19
  8.3 1.5 %collective-permute-start.1 = (bf16[32,4096]{1,0:T(8,128)(2,1)S(1)}, bf16[32,4096]{1,0:T(8,128)(2,1)S(1)}, u32[]{:S(2)}, u32[]{:S(2)}) collective-permute-start(bf16[32,4096]{1,0:T(8,128)(2,1)S(1)} %fusion.2.refs_0_), channel_id=1, source_target_pairs={{0,2},{2,0},{4,6},{6,4},{8,10},{10,8},{12,14},{14,12},{16,18},{18,... | collective-permute-start | bytes 786440 | tf_op jit(solution)/shard_map/ppermute | solution.py:19
  10.6 2.7 %collective-permute-start.5 = (bf16[32,4096]{1,0:T(8,128)(2,1)S(1)}, bf16[32,4096]{1,0:T(8,128)(2,1)S(1)}, u32[]{:S(2)}, u32[]{:S(2)}) collective-permute-start(bf16[32,4096]{1,0:T(8,128)(2,1)S(1)} %fusion.2.refs_0_), channel_id=1, source_target_pairs={{0,16},{2,18},{4,20},{6,22},{8,24},{10,26},{12,28},{14,30},{16,0},... | collective-permute-start | bytes 786440 | tf_op jit(solution)/shard_map/ppermute | solution.py:19
  13.3 2.0 %vocabulary_slices.1 = bf16[16,8,2000]{2,1,0:T(8,128)(2,1)} custom-call(bf16[8,32000]{1,0:T(8,128)(2,1)} %bitcast.17), custom_call_target="tpu_custom_call" | custom-call | bytes 1024000 | tf_op jit(solution)/shard_map/vocabulary_slices/pallas_call | solution.py:41
  15.3 1.1 %collective-permute-done.1.refs_1_ = bf16[32,4096]{1,0:T(8,128)(2,1)S(1)} collective-permute-done((bf16[32,4096]{1,0:T(8,128)(2,1)S(1)}, bf16[32,4096]{1,0:T(8,128)(2,1)S(1)}, u32[]{:S(2)}, u32[]{:S(2)}) %collective-permute-start.1) | collective-permute-done | bytes 262176 | tf_op jit(solution)/shard_map/ppermute | solution.py:19
  16.5 2.2 %collective-permute-start.4 = (bf16[32,4096]{1,0:T(8,128)(2,1)S(1)}, bf16[32,4096]{1,0:T(8,128)(2,1)S(1)}, u32[]{:S(2)}, u32[]{:S(2)}) collective-permute-start(bf16[32,4096]{1,0:T(8,128)(2,1)S(1)} %collective-permute-done.3.refs_4_), channel_id=1, source_target_pairs={{0,2},{2,0},{4,6},{6,4},{8,10},{10,8},{12,14},{14,12},{16,18},{18,... | collective-permute-start | bytes 786440 | tf_op jit(solution)/shard_map/ppermute | solution.py:19
  18.6 2.5 %collective-permute-start.11 = (bf16[32,4096]{1,0:T(8,128)(2,1)S(1)}, bf16[32,4096]{1,0:T(8,128)(2,1)S(1)}, u32[]{:S(2)}, u32[]{:S(2)}) collective-permute-start(bf16[32,4096]{1,0:T(8,128)(2,1)S(1)} %collective-permute-done.3.refs_4_), channel_id=1, source_target_pairs={{0,4},{2,6},{4,0},{6,2},{8,12},{10,14},{12,8},{14,10},{16,20},{18,... | collective-permute-start | bytes 786440 | tf_op jit(solution)/shard_map/ppermute | solution.py:19
  21.3 3.8 %collective-permute-done.5.refs_0_ = bf16[32,4096]{1,0:T(8,128)(2,1)S(1)} collective-permute-done((bf16[32,4096]{1,0:T(8,128)(2,1)S(1)}, bf16[32,4096]{1,0:T(8,128)(2,1)S(1)}, u32[]{:S(2)}, u32[]{:S(2)}) %collective-permute-start.5) | collective-permute-done | bytes 262176 | tf_op jit(solution)/shard_map/ppermute | solution.py:19
  25.8 2.5 %collective-permute-start.6 = (bf16[32,4096]{1,0:T(8,128)(2,1)S(1)}, bf16[32,4096]{1,0:T(8,128)(2,1)S(1)}, u32[]{:S(2)}, u32[]{:S(2)}) collective-permute-start(bf16[32,4096]{1,0:T(8,128)(2,1)S(1)} %collective-permute-done.4.refs_5_), channel_id=1, source_target_pairs={{0,4},{2,6},{4,0},{6,2},{8,12},{10,14},{12,8},{14,10},{16,20},{18,... | collective-permute-start | bytes 786440 | tf_op jit(solution)/shard_map/ppermute | solution.py:19
  28.3 2.1 %collective-permute-done.10.refs_3_ = bf16[32,4096]{1,0:T(8,128)(2,1)S(1)} collective-permute-done((bf16[32,4096]{1,0:T(8,128)(2,1)S(1)}, bf16[32,4096]{1,0:T(8,128)(2,1)S(1)}, u32[]{:S(2)}, u32[]{:S(2)}) %collective-permute-start.10) | collective-permute-done | bytes 262176 | tf_op jit(solution)/shard_map/ppermute | solution.py:19
  30.4 1.8 %collective-permute-start.13 = (bf16[32,4096]{1,0:T(8,128)(2,1)S(1)}, bf16[32,4096]{1,0:T(8,128)(2,1)S(1)}, u32[]{:S(2)}, u32[]{:S(2)}) collective-permute-start(bf16[32,4096]{1,0:T(8,128)(2,1)S(1)} %collective-permute-done.5.refs_0_), channel_id=1, source_target_pairs={{0,2},{2,0},{4,6},{6,4},{8,10},{10,8},{12,14},{14,12},{16,18},{18,... | collective-permute-start | bytes 786440 | tf_op jit(solution)/shard_map/ppermute | solution.py:19
  32.2 2.5 %collective-permute-start.12 = (bf16[32,4096]{1,0:T(8,128)(2,1)S(1)}, bf16[32,4096]{1,0:T(8,128)(2,1)}, u32[]{:S(2)}, u32[]{:S(2)}) collective-permute-start(bf16[32,4096]{1,0:T(8,128)(2,1)S(1)} %collective-permute-done.5.refs_0_), channel_id=1, source_target_pairs={{0,4},{2,6},{4,0},{6,2},{8,12},{10,14},{12,8},{14,10},{16,20},{18,... | collective-permute-start | bytes 786440 | tf_op jit(solution)/shard_map/ppermute | solution.py:19
  34.9 2.0 %collective-permute-start.8 = (bf16[32,4096]{1,0:T(8,128)(2,1)}, bf16[32,4096]{1,0:T(8,128)(2,1)}, u32[]{:S(2)}, u32[]{:S(2)}) collective-permute-start(bf16[32,4096]{1,0:T(8,128)(2,1)} %collective-permute-done.7.refs_4_), channel_id=1, source_target_pairs={{0,2},{2,0},{4,6},{6,4},{8,10},{10,8},{12,14},{14,12},{16,18},{18,... | collective-permute-start | bytes 786440 | tf_op jit(solution)/shard_map/ppermute | solution.py:19
  36.9 9.0 %multiply.5.refs_0_ = f32[2000,256]{1,0:T(8,128)S(1)} custom-call(s32[1]{0:T(128)} %bitcast.2.first_ref, bf16[32,4096]{1,0:T(8,128)(2,1)} %copy-done.4, bf16[32,4096]{1,0:T(8,128)(2,1)} %copy-done.8, bf16[32,4096]{1,0:T(8,128)(2,1)} %copy-done.7, bf16[32,4096]{1,0:T(8,128)(2,1)} %copy-done.13, bf16[32,4096]{1,0:T(8,128)(2,1)} %copy-done.6, ...), custom_call_target="tpu_custom_call" | custom-call | flops 16777216000 | bytes 65536000 | tf_op jit(solution)/shard_map/multiply/pallas_call | solution.py:120
  46.8 2.0 %collective-permute-start.15 = (bf16[32,4096]{1,0:T(8,128)(2,1)}, bf16[32,4096]{1,0:T(8,128)(2,1)S(1)}, u32[]{:S(2)}, u32[]{:S(2)}) collective-permute-start(bf16[32,4096]{1,0:T(8,128)(2,1)} %collective-permute-done.8.refs_5_), channel_id=1, source_target_pairs={{0,4},{2,6},{4,0},{6,2},{8,12},{10,14},{12,8},{14,10},{16,20},{18,... | collective-permute-start | bytes 786440 | tf_op jit(solution)/shard_map/ppermute | solution.py:19
  48.8 5.3 %all-to-all-start = ((bf16[16,8,2000]{2,1,0:T(8,128)(2,1)}), bf16[16,8,2000]{2,1,0:T(8,128)(2,1)}, u32[]{:S(2)}, u32[]{:S(2)}) async-start(bf16[16,8,2000]{2,1,0:T(8,128)(2,1)} %vocabulary_slices.1), calls=%async_computation | async-start | bytes 1048576 | tf_op jit(solution)/shard_map/all_to_all | solution.py:328
  57.0 8.3 %multiply.6 = (f32[1200,256]{1,0:T(8,128)}, f32[800,256]{1,0:T(8,128)S(1)}) custom-call(s32[1]{0:T(128)} %bitcast.2.first_ref, bf16[32,4096]{1,0:T(8,128)(2,1)} %copy-done.5, bf16[32,4096]{1,0:T(8,128)(2,1)} %copy-done.9, bf16[32,4096]{1,0:T(8,128)(2,1)} %collective-permute-done.12.refs_2_, bf16[32,4096]{1,0:T(8,128)(2,1)S(1)} %collective-permute-done.14.refs_3_, ...), custom_call_target="tpu_custom_call" | custom-call | flops 16777216000 | bytes 65536000 | tf_op jit(solution)/shard_map/multiply/pallas_call | solution.py:120
  65.4 3.4 %all-to-all-done = bf16[16,8,2000]{2,1,0:T(8,128)(2,1)} async-done(((bf16[16,8,2000]{2,1,0:T(8,128)(2,1)}), bf16[16,8,2000]{2,1,0:T(8,128)(2,1)}, u32[]{:S(2)}, u32[]{:S(2)}) %all-to-all-start) | async-done | bytes 512032 | tf_op jit(solution)/shard_map/all_to_all | solution.py:328
  68.8 1.3 %copy.17 = bf16[128,2000]{0,1:T(8,128)(2,1)S(1)} copy(bf16[128,2000]{1,0:T(8,128)(2,1)} %bitcast.4) | data formatting | bytes 1024000 | tf_op jit(solution)/shard_map/reshape | solution.py:336
  70.7 1.7 %collective-permute-done.19 = bf16[128,2000]{0,1:T(8,128)(2,1)} collective-permute-done((bf16[128,2000]{0,1:T(8,128)(2,1)S(1)}, bf16[128,2000]{0,1:T(8,128)(2,1)}, u32[]{:S(2)}, u32[]{:S(2)}) %collective-permute-start.19) | collective-permute-done | bytes 512032 | tf_op jit(solution)/shard_map/ppermute | solution.py:19
  72.3 4.3 %statistics.1 = (f32[2000,256]{1,0:T(8,128)S(1)}, f32[16,2,256]{2,1,0:T(2,128)S(1)}) custom-call(s32[1]{0:T(128)} %bitcast.late_ref, f32[2000,256]{1,0:T(8,128)} %copy-done, f32[2000,256]{1,0:T(8,128)} %collective-permute-done.16.refs_1_, f32[1200,256]{1,0:T(8,128)} %get-tuple-element.56.refs_2_, f32[800,256]{1,0:T(8,128)} %copy-done.1, ...), custom_call_target="tpu_custom_call" | custom-call | flops 2048000 | bytes 8192000 | tf_op jit(solution)/shard_map/statistics/pallas_call | solution.py:216
  76.7 11.4 %all_to_all.10.arrived_hbm = f32[16,2,256]{2,1,0:T(2,128)S(1)} all-to-all(f32[16,2,256]{2,1,0:T(2,128)S(1)} %get-tuple-element.64), channel_id=1, replica_groups=mesh['wide'=16,'narrow'=2] {'wide'}, dimensions={0} | all-to-all | bytes 65536 | tf_op jit(solution)/shard_map/all_to_all | solution.py:339
  88.1 2.5 %subtract.2 = f32[2000,256]{1,0:T(8,128)} custom-call(f32[2000,256]{1,0:T(8,128)S(1)} %get-tuple-element.63.total_hbm, f32[16,2,256]{2,1,0:T(2,128)S(1)} %all_to_all.10.arrived_hbm), custom_call_target="tpu_custom_call" | custom-call | flops 512000 | bytes 4096000 | tf_op jit(solution)/shard_map/subtract/pallas_call | solution.py:268
  (69 shorter events, 10.2 us)
Async XLA Ops:
  1.1 1.9 %collective-permute-start = (f32[32]{0:T(128)S(1)}, f32[32]{0:T(128)S(1)}, u32[]{:S(2)}, u32[]{:S(2)}) collective-permute-start(f32[32]{0:T(128)S(1)} %fusion), channel_id=1, source_target_pairs={{0,1},{1,0},{2,3},{3,2},{4,5},{5,4},{6,7},{7,6},{8,9},{9,8},{10,11... | collective-permute-start | bytes 392 | tf_op jit(solution)/shard_map/ppermute | solution.py:19
  4.1 32.8 %copy-start.4 = (bf16[32,4096]{1,0:T(8,128)(2,1)}, bf16[32,4096]{1,0:T(8,128)(2,1)S(1)}, u32[]{:S(2)}) copy-start(bf16[32,4096]{1,0:T(8,128)(2,1)S(1)} %fusion.2.refs_0_) | copy-start | bytes 786436
  4.1 11.2 %collective-permute-start.3 = (bf16[32,4096]{1,0:T(8,128)(2,1)S(1)}, bf16[32,4096]{1,0:T(8,128)(2,1)S(1)}, u32[]{:S(2)}, u32[]{:S(2)}) collective-permute-start(bf16[32,4096]{1,0:T(8,128)(2,1)S(1)} %fusion.2.refs_0_), channel_id=1, source_target_pairs={{0,8},{2,10},{4,12},{6,14},{8,0},{10,2},{12,4},{14,6},{16,24},{18,... | collective-permute-start | bytes 786440 | tf_op jit(solution)/shard_map/ppermute | solution.py:19
  6.8 8.5 %collective-permute-start.2 = (bf16[32,4096]{1,0:T(8,128)(2,1)S(1)}, bf16[32,4096]{1,0:T(8,128)(2,1)S(1)}, u32[]{:S(2)}, u32[]{:S(2)}) collective-permute-start(bf16[32,4096]{1,0:T(8,128)(2,1)S(1)} %fusion.2.refs_0_), channel_id=1, source_target_pairs={{0,4},{2,6},{4,0},{6,2},{8,12},{10,14},{12,8},{14,10},{16,20},{18,... | collective-permute-start | bytes 786440 | tf_op jit(solution)/shard_map/ppermute | solution.py:19
  8.3 8.1 %collective-permute-start.1 = (bf16[32,4096]{1,0:T(8,128)(2,1)S(1)}, bf16[32,4096]{1,0:T(8,128)(2,1)S(1)}, u32[]{:S(2)}, u32[]{:S(2)}) collective-permute-start(bf16[32,4096]{1,0:T(8,128)(2,1)S(1)} %fusion.2.refs_0_), channel_id=1, source_target_pairs={{0,2},{2,0},{4,6},{6,4},{8,10},{10,8},{12,14},{14,12},{16,18},{18,... | collective-permute-start | bytes 786440 | tf_op jit(solution)/shard_map/ppermute | solution.py:19
  10.6 14.4 %collective-permute-start.5 = (bf16[32,4096]{1,0:T(8,128)(2,1)S(1)}, bf16[32,4096]{1,0:T(8,128)(2,1)S(1)}, u32[]{:S(2)}, u32[]{:S(2)}) collective-permute-start(bf16[32,4096]{1,0:T(8,128)(2,1)S(1)} %fusion.2.refs_0_), channel_id=1, source_target_pairs={{0,16},{2,18},{4,20},{6,22},{8,24},{10,26},{12,28},{14,30},{16,0},... | collective-permute-start | bytes 786440 | tf_op jit(solution)/shard_map/ppermute | solution.py:19
  15.3 21.6 %copy-start.6 = (bf16[32,4096]{1,0:T(8,128)(2,1)}, bf16[32,4096]{1,0:T(8,128)(2,1)S(1)}, u32[]{:S(2)}) copy-start(bf16[32,4096]{1,0:T(8,128)(2,1)S(1)} %collective-permute-done.3.refs_4_) | copy-start | bytes 786436
  15.3 21.5 %copy-start.7 = (bf16[32,4096]{1,0:T(8,128)(2,1)}, bf16[32,4096]{1,0:T(8,128)(2,1)S(1)}, u32[]{:S(2)}) copy-start(bf16[32,4096]{1,0:T(8,128)(2,1)S(1)} %collective-permute-done.2.refs_2_) | copy-start | bytes 786436
  16.5 9.3 %collective-permute-start.4 = (bf16[32,4096]{1,0:T(8,128)(2,1)S(1)}, bf16[32,4096]{1,0:T(8,128)(2,1)S(1)}, u32[]{:S(2)}, u32[]{:S(2)}) collective-permute-start(bf16[32,4096]{1,0:T(8,128)(2,1)S(1)} %collective-permute-done.3.refs_4_), channel_id=1, source_target_pairs={{0,2},{2,0},{4,6},{6,4},{8,10},{10,8},{12,14},{14,12},{16,18},{18,... | collective-permute-start | bytes 786440 | tf_op jit(solution)/shard_map/ppermute | solution.py:19
  18.6 11.8 %collective-permute-start.11 = (bf16[32,4096]{1,0:T(8,128)(2,1)S(1)}, bf16[32,4096]{1,0:T(8,128)(2,1)S(1)}, u32[]{:S(2)}, u32[]{:S(2)}) collective-permute-start(bf16[32,4096]{1,0:T(8,128)(2,1)S(1)} %collective-permute-done.3.refs_4_), channel_id=1, source_target_pairs={{0,4},{2,6},{4,0},{6,2},{8,12},{10,14},{12,8},{14,10},{16,20},{18,... | collective-permute-start | bytes 786440 | tf_op jit(solution)/shard_map/ppermute | solution.py:19
  21.2 9.3 %collective-permute-start.10 = (bf16[32,4096]{1,0:T(8,128)(2,1)S(1)}, bf16[32,4096]{1,0:T(8,128)(2,1)S(1)}, u32[]{:S(2)}, u32[]{:S(2)}) collective-permute-start(bf16[32,4096]{1,0:T(8,128)(2,1)S(1)} %collective-permute-done.2.refs_2_), channel_id=1, source_target_pairs={{0,2},{2,0},{4,6},{6,4},{8,10},{10,8},{12,14},{14,12},{16,18},{18,... | collective-permute-start | bytes 786440 | tf_op jit(solution)/shard_map/ppermute | solution.py:19
  25.8 9.0 %collective-permute-start.6 = (bf16[32,4096]{1,0:T(8,128)(2,1)S(1)}, bf16[32,4096]{1,0:T(8,128)(2,1)S(1)}, u32[]{:S(2)}, u32[]{:S(2)}) collective-permute-start(bf16[32,4096]{1,0:T(8,128)(2,1)S(1)} %collective-permute-done.4.refs_5_), channel_id=1, source_target_pairs={{0,4},{2,6},{4,0},{6,2},{8,12},{10,14},{12,8},{14,10},{16,20},{18,... | collective-permute-start | bytes 786440 | tf_op jit(solution)/shard_map/ppermute | solution.py:19
  28.3 6.5 %collective-permute-start.7 = (bf16[32,4096]{1,0:T(8,128)(2,1)S(1)}, bf16[32,4096]{1,0:T(8,128)(2,1)}, u32[]{:S(2)}, u32[]{:S(2)}) collective-permute-start(bf16[32,4096]{1,0:T(8,128)(2,1)S(1)} %collective-permute-done.5.refs_0_), channel_id=1, source_target_pairs={{0,8},{2,10},{4,12},{6,14},{8,0},{10,2},{12,4},{14,6},{16,24},{18,... | collective-permute-start | bytes 786440 | tf_op jit(solution)/shard_map/ppermute | solution.py:19
  30.4 15.5 %collective-permute-start.13 = (bf16[32,4096]{1,0:T(8,128)(2,1)S(1)}, bf16[32,4096]{1,0:T(8,128)(2,1)S(1)}, u32[]{:S(2)}, u32[]{:S(2)}) collective-permute-start(bf16[32,4096]{1,0:T(8,128)(2,1)S(1)} %collective-permute-done.5.refs_0_), channel_id=1, source_target_pairs={{0,2},{2,0},{4,6},{6,4},{8,10},{10,8},{12,14},{14,12},{16,18},{18,... | collective-permute-start | bytes 786440 | tf_op jit(solution)/shard_map/ppermute | solution.py:19
  32.2 13.7 %collective-permute-start.12 = (bf16[32,4096]{1,0:T(8,128)(2,1)S(1)}, bf16[32,4096]{1,0:T(8,128)(2,1)}, u32[]{:S(2)}, u32[]{:S(2)}) collective-permute-start(bf16[32,4096]{1,0:T(8,128)(2,1)S(1)} %collective-permute-done.5.refs_0_), channel_id=1, source_target_pairs={{0,4},{2,6},{4,0},{6,2},{8,12},{10,14},{12,8},{14,10},{16,20},{18,... | collective-permute-start | bytes 786440 | tf_op jit(solution)/shard_map/ppermute | solution.py:19
  34.8 11.2 %collective-permute-start.9 = (bf16[32,4096]{1,0:T(8,128)(2,1)}, bf16[32,4096]{1,0:T(8,128)(2,1)S(1)}, u32[]{:S(2)}, u32[]{:S(2)}) collective-permute-start(bf16[32,4096]{1,0:T(8,128)(2,1)} %collective-permute-done.7.refs_4_), channel_id=1, source_target_pairs={{0,4},{2,6},{4,0},{6,2},{8,12},{10,14},{12,8},{14,10},{16,20},{18,... | collective-permute-start | bytes 786440 | tf_op jit(solution)/shard_map/ppermute | solution.py:19
  34.9 11.1 %collective-permute-start.8 = (bf16[32,4096]{1,0:T(8,128)(2,1)}, bf16[32,4096]{1,0:T(8,128)(2,1)}, u32[]{:S(2)}, u32[]{:S(2)}) collective-permute-start(bf16[32,4096]{1,0:T(8,128)(2,1)} %collective-permute-done.7.refs_4_), channel_id=1, source_target_pairs={{0,2},{2,0},{4,6},{6,4},{8,10},{10,8},{12,14},{14,12},{16,18},{18,... | collective-permute-start | bytes 786440 | tf_op jit(solution)/shard_map/ppermute | solution.py:19
  46.0 10.1 %collective-permute-start.16 = (f32[2000,256]{1,0:T(8,128)S(1)}, f32[2000,256]{1,0:T(8,128)}, u32[]{:S(2)}, u32[]{:S(2)}) collective-permute-start(f32[2000,256]{1,0:T(8,128)S(1)} %multiply.5.refs_0_), channel_id=1, source_target_pairs={{0,1},{1,0},{2,3},{3,2},{4,5},{5,4},{6,7},{7,6},{8,9},{9,8},{10,11... | collective-permute-start | bytes 6144008 | tf_op jit(solution)/shard_map/ppermute | solution.py:19
  46.7 8.3 %collective-permute-start.14 = (bf16[32,4096]{1,0:T(8,128)(2,1)}, bf16[32,4096]{1,0:T(8,128)(2,1)S(1)}, u32[]{:S(2)}, u32[]{:S(2)}) collective-permute-start(bf16[32,4096]{1,0:T(8,128)(2,1)} %collective-permute-done.12.refs_2_), channel_id=1, source_target_pairs={{0,2},{2,0},{4,6},{6,4},{8,10},{10,8},{12,14},{14,12},{16,18},{18,... | collective-permute-start | bytes 786440 | tf_op jit(solution)/shard_map/ppermute | solution.py:19
  46.8 8.6 %collective-permute-start.15 = (bf16[32,4096]{1,0:T(8,128)(2,1)}, bf16[32,4096]{1,0:T(8,128)(2,1)S(1)}, u32[]{:S(2)}, u32[]{:S(2)}) collective-permute-start(bf16[32,4096]{1,0:T(8,128)(2,1)} %collective-permute-done.8.refs_5_), channel_id=1, source_target_pairs={{0,4},{2,6},{4,0},{6,2},{8,12},{10,14},{12,8},{14,10},{16,20},{18,... | collective-permute-start | bytes 786440 | tf_op jit(solution)/shard_map/ppermute | solution.py:19
  48.8 20.0 %all-to-all-start = ((bf16[16,8,2000]{2,1,0:T(8,128)(2,1)}), bf16[16,8,2000]{2,1,0:T(8,128)(2,1)}, u32[]{:S(2)}, u32[]{:S(2)}) async-start(bf16[16,8,2000]{2,1,0:T(8,128)(2,1)} %vocabulary_slices.1), calls=%async_computation | async-start | bytes 1048576 | tf_op jit(solution)/shard_map/all_to_all | solution.py:328
  65.3 7.0 %collective-permute-start.17 = (f32[1200,256]{1,0:T(8,128)}, f32[1200,256]{1,0:T(8,128)S(1)}, u32[]{:S(2)}, u32[]{:S(2)}) collective-permute-start(f32[1200,256]{1,0:T(8,128)} %get-tuple-element.56.refs_2_), channel_id=1, source_target_pairs={{0,1},{1,0},{2,3},{3,2},{4,5},{5,4},{6,7},{7,6},{8,9},{9,8},{10,11... | collective-permute-start | bytes 3686408 | tf_op jit(solution)/shard_map/ppermute | solution.py:19
  68.8 3.6 %collective-permute-start.18 = (f32[800,256]{1,0:T(8,128)S(1)}, f32[800,256]{1,0:T(8,128)S(1)}, u32[]{:S(2)}, u32[]{:S(2)}) collective-permute-start(f32[800,256]{1,0:T(8,128)S(1)} %get-tuple-element.59.refs_3_), channel_id=1, source_target_pairs={{0,1},{1,0},{2,3},{3,2},{4,5},{5,4},{6,7},{7,6},{8,9},{9,8},{10,11... | collective-permute-start | bytes 2457608 | tf_op jit(solution)/shard_map/ppermute | solution.py:19
  70.1 2.2 %collective-permute-start.19 = (bf16[128,2000]{0,1:T(8,128)(2,1)S(1)}, bf16[128,2000]{0,1:T(8,128)(2,1)}, u32[]{:S(2)}, u32[]{:S(2)}) collective-permute-start(bf16[128,2000]{0,1:T(8,128)(2,1)S(1)} %copy.17), channel_id=1, source_target_pairs={{0,1},{1,0},{2,3},{3,2},{4,5},{5,4},{6,7},{7,6},{8,9},{9,8},{10,11... | collective-permute-start | bytes 1536008 | tf_op jit(solution)/shard_map/ppermute | solution.py:19
  (11 other events, 94.8 us)
